TPU v7x, 512 devices: a whole 4x4x16 slice. The times are simulated.
512 devices in a mesh: lat: 32 (over z, core), tp: 16 (over x, y).
Axes of the slice: x: 4, y: 4, z: 16, core: 2. Of those that a mesh axis runs over, the one named last changes fastest.
Arguments:
- activations: bfloat16 [256, 3584], P(None, 'lat'), may hold values from -6 to 6
- indices: int32 [256, 64], replicated, may hold values from 0 to 65535
- w_enc: bfloat16 [3584, 65536], P(None, ('lat', 'tp')), may hold values from -0.09375 to 0.09375
- b_enc: float32 [65536], P(('lat', 'tp')), may hold values from -5 to 5
- w_dec: bfloat16 [65536, 3584], P(('lat', 'tp')), may hold values from -3 to 3
- b_dec: float32 [3584], P('lat'), may hold values from -3 to 3
- w_gate: bfloat16 [3584, 14336], P('lat', 'tp'), may hold values from -0.09375 to 0.09375
- w_up: bfloat16 [3584, 14336], P('lat', 'tp'), may hold values from -0.09375 to 0.09375
- w_down: bfloat16 [14336, 3584], P('tp', 'lat'), may hold values from -0.046875 to 0.046875
- cotangent: bfloat16 [256, 3584], P(None, 'lat'), may hold values from -6 to 6
Outputs:
- output: bfloat16 [256, 3584], P('tp', 'lat')
- grad_enc: bfloat16 [3584, 65536], P(None, ('lat', 'tp'))
- grad_enc_bias: float32 [65536], P(('lat', 'tp'))
- grad_dec: bfloat16 [65536, 3584], P(('lat', 'tp'))
- grad_dec_bias: float32 [3584], P('lat')
Inputs may be any that keep to these rules, and one draw needn't show every extreme that they name: `indices`: each row names 64 latents; a latent named more than once in a row counts once; some latents are named far more often than others.
All inputs are finite; a program needn't handle non-finite values.
Results may differ from a plain program's by a relative error of at most 0.011.
Values may be sent and summed in bfloat16 or wider, within the bound.
A program may use at most 64 MiB of HBM per device.

v0:
```python
import jax
import jax.numpy as jnp
from jax import lax
from jax.sharding import PartitionSpec as P


def gelu_parts(value):
    coeff = 0.7978845608028654
    inner = coeff * (value + 0.044715 * value * value * value)
    tanh_term = jnp.tanh(inner)
    gelu_value = 0.5 * value * (1.0 + tanh_term)
    slope = 0.5 * (1.0 + tanh_term) + 0.5 * value * (1.0 - tanh_term * tanh_term) * coeff * (
        1.0 + 3.0 * 0.044715 * value * value
    )
    return (gelu_value, slope)


def contract_rows(left, right):
    return lax.dot_general(
        left, right, (((0,), (0,)), ((), ())), preferred_element_type=jnp.float32
    )


def contract_cols(left, right):
    return lax.dot_general(
        left, right, (((1,), (1,)), ((), ())), preferred_element_type=jnp.float32
    )


def on_device(activations, indices, w_enc, b_enc, w_dec, b_dec, w_gate, w_up, w_down, cotangent):
    n_tp = lax.axis_size("tp")
    lat_dev = w_enc.shape[1]
    rows = activations.shape[0]
    width = activations.shape[1]
    own_rows = rows // n_tp
    row_start = lax.axis_index("tp") * own_rows
    shard = lax.axis_index("lat") * n_tp + lax.axis_index("tp")
    columns = shard * lat_dev + jnp.arange(lat_dev, dtype=jnp.int32)
    hit = jnp.any(indices[:, :, None] == columns[None, None, :], axis=1).astype(jnp.float32)
    inputs = lax.all_gather(activations, "lat", axis=1, tiled=True)
    pre = jnp.dot(inputs, w_enc, preferred_element_type=jnp.float32) + b_enc
    act = (pre * hit).astype(jnp.bfloat16)
    partial_value = jnp.dot(act, w_dec, preferred_element_type=jnp.float32)
    summed_lat = lax.psum_scatter(partial_value, "lat", scatter_dimension=1, tiled=True)
    recon = (lax.psum(summed_lat, "tp") + b_dec).astype(jnp.bfloat16)
    gate, up = lax.psum(
        (
            jnp.dot(recon, w_gate, preferred_element_type=jnp.float32),
            jnp.dot(recon, w_up, preferred_element_type=jnp.float32),
        ),
        "lat",
    )
    gelu_value, slope = gelu_parts(gate)
    hidden = (gelu_value * up).astype(jnp.bfloat16)
    down = jnp.dot(hidden, w_down, preferred_element_type=jnp.float32)
    mixed = lax.psum_scatter(down, "tp", scatter_dimension=0, tiled=True)
    recon_own = lax.dynamic_slice_in_dim(recon, row_start, own_rows, 0)
    output = (recon_own.astype(jnp.float32) + mixed).astype(jnp.bfloat16)
    back_hidden = lax.psum(contract_cols(cotangent, w_down), "lat")
    back_gate = (back_hidden * up * slope).astype(jnp.bfloat16)
    back_up = (back_hidden * gelu_value).astype(jnp.bfloat16)
    through = contract_cols(back_gate, w_gate) + contract_cols(back_up, w_up)
    through_total = lax.psum(through, "tp")
    back_local = (
        cotangent.astype(jnp.float32)
        + through_total
        + recon.astype(jnp.float32)
        - activations.astype(jnp.float32)
    ).astype(jnp.bfloat16)
    back_full = lax.all_gather(back_local, "lat", axis=1, tiled=True)
    back_cols = lax.dynamic_slice_in_dim(back_full, lax.axis_index("lat") * width, width, 1)
    grad_dec_bias = jnp.sum(back_cols.astype(jnp.float32), axis=0)
    back_act = (contract_cols(back_full, w_dec) * hit).astype(jnp.bfloat16)
    grad_dec = contract_rows(act, back_full).astype(jnp.bfloat16)
    grad_enc = contract_rows(inputs, back_act).astype(jnp.bfloat16)
    grad_enc_bias = jnp.sum(back_act.astype(jnp.float32), axis=0)
    return (output, grad_enc, grad_enc_bias, grad_dec, grad_dec_bias)


def solution(mesh):
    return jax.shard_map(
        on_device,
        mesh=mesh,
        in_specs=(
            P(None, "lat"),
            P(),
            P(None, ("lat", "tp")),
            P(("lat", "tp")),
            P(("lat", "tp"), None),
            P("lat"),
            P("lat", "tp"),
            P("lat", "tp"),
            P("tp", "lat"),
            P(None, "lat"),
        ),
        out_specs=(
            P("tp", "lat"),
            P(None, ("lat", "tp")),
            P(("lat", "tp")),
            P(("lat", "tp"), None),
            P("lat"),
        ),
        check_vma=False,
    )
```

profile of v0, /device:TPU:1, one launch (start us, length us, event | category | flops | bytes accessed | tf_op | source)
XLA Modules:
  0.0 746.3 jit_solution(8785803412892001758)
XLA Ops:
  7.2 0.0 copy-start
  7.2 0.0 all-gather.3.cloned.1.call-start
  7.2 0.7 all-gather.3.cloned.1.call-update
  7.9 0.0 reduce-scatter.3.cloned.1.call-start
  8.0 0.9 copy.23
  8.9 2.8 compare_reduce_fusion
  11.7 75.7 %all-gather.3.cloned.1.call-done = bf16[256,3584]{0,1:T(8,128)(2,1)} async-done(((bf16[256,112]{0,1:T(8,128)(2,1)}), bf16[256,3584]{0,1:T(8,128)(2,1)}) %all-gather.3.cloned.1.call-update) | async-done | bytes 1835024 | tf_op jit(solution)/shard_map/all_gather | solution.py:40
  87.4 2.5 fusion.2
  89.9 0.0 copy-done
  89.9 2.5 fusion.28
  92.4 0.0 copy-start.4
  92.4 0.0 copy-start.5
  92.4 0.0 copy-start.8
  92.4 0.0 copy-start.6
  92.4 0.0 reduce-scatter.3.cloned.1.call-update
  92.5 0.0 copy-start.7
  92.5 0.0 all-reduce.7.cloned.1.call-start
  92.5 106.0 %reduce-scatter.3.cloned.1.call-done = f32[256,112]{0,1:T(8,128)} async-done(((f32[256,3584]{0,1:T(8,128)}), f32[256,112]{0,1:T(8,128)}) %reduce-scatter.3.cloned.1.call-update) | async-done | bytes 114704 | tf_op jit(solution)/shard_map/reduce_scatter | solution.py:44
  198.6 0.0 all-reduce.7.cloned.1.call-update
  198.6 0.0 all-reduce.9.cloned.1.call-start
  198.6 0.0 copy-done.4
  198.6 0.0 copy-done.5
  198.7 1.2 fusion.31
  199.9 114.3 %all-reduce.7.cloned.1.call-done = f32[256,112]{0,1:T(8,128)} async-done(((f32[256,112]{0,1:T(8,128)}), f32[256,112]{0,1:T(8,128)}) %all-reduce.7.cloned.1.call-update) | async-done | bytes 114704 | tf_op jit(solution)/shard_map/psum | solution.py:45
  314.2 0.0 copy-done.8
  314.2 1.0 add_convert_fusion
  315.2 0.0 copy-done.6
  315.2 1.2 fusion.29
  316.4 0.0 copy-done.7
  316.4 1.2 fusion.30
  317.7 0.0 all-reduce.9.cloned.1.call-update
  317.7 0.0 all-reduce.11.cloned.1.call-start
  317.7 216.4 %all-reduce.9.cloned.1.call-done = (f32[256,896]{1,0:T(8,128)}, f32[256,896]{1,0:T(8,128)}, f32[256,896]{1,0:T(8,128)}) async-done(((f32[256,896]{1,0:T(8,128)}, f32[256,896]{1,0:T(8,128)}, f32[256,896]{1,0:T(8,128)}), (f32[256,896]{1,0:T(8,128)}, f32[256,896]{1,0:T(8,128)}, f32[256,896]{1,0:T(8,128)})) %all-reduce.9.cloned.1.call-update) | async-done | bytes 2752528 | tf_op jit(solution)/shard_map/psum | solution.py:46
  534.2 0.0 copy-start.9
  534.2 0.0 copy-start.10
  534.2 0.0 copy-start.11
  534.2 2.7 fusion.11
  536.9 0.0 copy-done.9
  536.9 0.0 copy-done.10
  536.9 0.0 copy-done.11
  536.9 0.8 fusion.12
  537.7 0.0 copy-start.2
  537.7 0.0 copy-start.3
  537.7 1.1 convolution_add_fusion.1
  538.8 0.0 all-reduce.11.cloned.1.call-update
  538.9 0.0 all-gather.5.cloned.1.call-start
  538.9 114.5 %all-reduce.11.cloned.1.call-done = (f32[256,112]{0,1:T(8,128)}, f32[256,112]{0,1:T(8,128)}) async-done(((f32[256,112]{0,1:T(8,128)}, f32[256,112]{0,1:T(8,128)}), (f32[256,112]{0,1:T(8,128)}, f32[256,112]{0,1:T(8,128)})) %all-reduce.11.cloned.1.call-update) | async-done | bytes 229392
  653.4 0.0 copy-done.2
  653.4 0.0 copy-done.3
  653.4 1.6 subtract_convert_fusion
  655.0 0.0 all-gather.5.cloned.1.call-update
  655.0 1.3 dynamic-slice
  657.0 0.9 fusion.14
  657.9 0.7 copy.25
  658.6 70.4 %all-gather.5.cloned.1.call-done = bf16[256,3584]{0,1:T(8,128)(2,1)} async-done(((bf16[256,112]{0,1:T(8,128)(2,1)}), bf16[256,3584]{0,1:T(8,128)(2,1)}) %all-gather.5.cloned.1.call-update) | async-done | bytes 1835024 | tf_op jit(solution)/shard_map/all_gather | solution.py:70
  728.9 2.7 convert_reduce_fusion
  731.7 0.0 copy-start.1
  731.7 3.3 fusion
  735.0 2.2 copy.26
  737.2 0.0 copy-done.1
  737.2 1.7 convolution_convert_fusion
  738.8 0.6 convert_reduce_fusion.1
  (1 shorter events, 0.0 us)
Async XLA Ops:
  7.2 82.8 %copy-start = (bf16[128,3584]{1,0:T(8,128)(2,1)S(1)}, bf16[128,3584]{1,0:T(8,128)(2,1)}, u32[]{:S(2)}) copy-start(bf16[128,3584]{1,0:T(8,128)(2,1)} %param.14) | copy-start | bytes 2752516
  7.2 80.3 %all-gather.3.cloned.1.call-start = ((), (), s32[]{:S(2)}) async-start(), calls=%async_computation.1 | async-start | bytes 1892352 | tf_op jit(solution)/shard_map/all_gather | solution.py:40
  7.9 190.6 %reduce-scatter.3.cloned.1.call-start = ((), (), s32[]{:S(2)}) async-start(), calls=%async_computation.2 | async-start | bytes 3784704 | tf_op jit(solution)/shard_map/reduce_scatter | solution.py:44
  92.4 106.2 %copy-start.4 = (bf16[256,112]{0,1:T(8,128)(2,1)S(1)}, bf16[256,112]{0,1:T(8,128)(2,1)}, u32[]{:S(2)}) copy-start(bf16[256,112]{0,1:T(8,128)(2,1)} %param.19) | copy-start | bytes 172036
  92.4 106.2 %copy-start.5 = (bf16[896,112]{0,1:T(8,128)(2,1)S(1)}, bf16[896,112]{0,1:T(8,128)(2,1)}, u32[]{:S(2)}) copy-start(bf16[896,112]{0,1:T(8,128)(2,1)} %param.18) | copy-start | bytes 602116
  92.4 221.8 %copy-start.8 = (f32[112]{0:T(128)S(1)}, f32[112]{0:T(128)}, u32[]{:S(2)}) copy-start(f32[112]{0:T(128)} %param.15) | copy-start | bytes 1348
  92.4 222.7 %copy-start.6 = (bf16[112,896]{1,0:T(8,128)(2,1)S(1)}, bf16[112,896]{1,0:T(8,128)(2,1)}, u32[]{:S(2)}) copy-start(bf16[112,896]{1,0:T(8,128)(2,1)} %param.16) | copy-start | bytes 602116
  92.5 224.0 %copy-start.7 = (bf16[112,896]{1,0:T(8,128)(2,1)S(1)}, bf16[112,896]{1,0:T(8,128)(2,1)}, u32[]{:S(2)}) copy-start(bf16[112,896]{1,0:T(8,128)(2,1)} %param.17) | copy-start | bytes 602116
  92.5 221.7 %all-reduce.7.cloned.1.call-start = ((), (), s32[]{:S(2)}) async-start(), calls=%async_computation.3 | async-start | bytes 229376 | tf_op jit(solution)/shard_map/psum | solution.py:45
  198.6 335.6 %all-reduce.9.cloned.1.call-start = ((), (), s32[]{:S(2)}) async-start(), calls=%async_computation.5 | async-start | bytes 5505024 | tf_op jit(solution)/shard_map/psum | solution.py:46
  317.7 335.7 %all-reduce.11.cloned.1.call-start = ((), (), s32[]{:S(2)}) async-start(), calls=%async_computation.6 | async-start | bytes 458752
  534.2 2.7 copy-start.9
  534.2 2.7 copy-start.10
  534.2 2.7 copy-start.11
  537.7 115.7 %copy-start.2 = (f32[256,112]{0,1:T(8,128)S(1)}, f32[256,112]{0,1:T(8,128)}, u32[]{:S(2)}) copy-start(f32[256,112]{0,1:T(8,128)} %all-reduce.7.cloned.1.call-done) | copy-start | bytes 344068
  537.7 115.7 %copy-start.3 = (bf16[256,112]{0,1:T(8,128)(2,1)S(1)}, bf16[256,112]{0,1:T(8,128)(2,1)}, u32[]{:S(2)}) copy-start(bf16[256,112]{0,1:T(8,128)(2,1)} %param.10) | copy-start | bytes 172036
  538.9 190.1 %all-gather.5.cloned.1.call-start = ((), (), s32[]{:S(2)}) async-start(), calls=%async_computation.4 | async-start | bytes 1892352 | tf_op jit(solution)/shard_map/all_gather | solution.py:70
  731.7 5.5 copy-start.1
Sparse Core Ops, SparseCore 0:
  10.1 77.2 all-gather.2
  92.6 105.9 reduce-scatter.2
  202.1 112.0 all-reduce.6
  317.8 216.3 all-reduce.8
  539.0 114.3 all-reduce.10
  656.2 72.7 all-gather.4
where the time goes:
time: 747 us; the launch traced here: 746 us
  waiting for transfers between devices  698 us (93%)
  matrix products  21 us (3%)
  between operations  14.9 us (2%)
    psum x1, waiting for transfers between devices, on_device(): lax.psum((jnp.dot(recon, w_gate, preferred_element_type=jnp.float32), jnp...  216 us
    unnamed x7, waiting for transfers between devices  115 us
    psum x1, waiting for transfers between devices, on_device(): recon = (lax.psum(summed_lat, 'tp') + b_dec).astype(jnp.bfloat16)  114 us
    reduce_scatter x1, waiting for transfers between devices, on_device(): lax.psum_scatter(partial_value, 'lat', scatter_dimension=1, tiled=True)  106 us
    all_gather x1, waiting for transfers between devices, on_device(): inputs = lax.all_gather(activations, 'lat', axis=1, tiled=True)  75.7 us
    all_gather x1, waiting for transfers between devices, on_device(): back_full = lax.all_gather(back_local, 'lat', axis=1, tiled=True)  70.4 us
  transfers between devices with their start and end apart: 6, of which 6 were waited for; matrix products, arithmetic and copies ran while one was open for 1% of the time, Pallas kernels for 0%

commit v1 on v0

v1 whole, which is shorter than its diff:
```python
import functools

import jax
import jax.numpy as jnp
from jax import lax
from jax.experimental import pallas as pl
from jax.experimental.pallas import tpu as pltpu
from jax.sharding import PartitionSpec as P

MESH = pl.DeviceIdType.MESH
NZ = 16
NT = 16
PAIR = 1
MEM = 2 * PAIR
NP = NZ // PAIR
TB = NT // MEM
RB = 16 * TB
W = 112
FF = 896
BF = jnp.bfloat16
F32 = jnp.float32


def mm(a, b):
    return lax.dot_general(a, b, (((1,), (0,)), ((), ())), preferred_element_type=F32)


def mm_nt(a, b):
    return lax.dot_general(a, b, (((1,), (1,)), ((), ())), preferred_element_type=F32)


def mm_tn(a, b):
    return lax.dot_general(a, b, (((0,), (0,)), ((), ())), preferred_element_type=F32)


def gelu_parts(value):
    coeff = 0.7978845608028654
    inner = coeff * (value + 0.044715 * value * value * value)
    tanh_term = jnp.tanh(inner)
    gelu_value = 0.5 * value * (1.0 + tanh_term)
    slope = 0.5 * (1.0 + tanh_term) + 0.5 * value * (1.0 - tanh_term * tanh_term) * coeff * (
        1.0 + 3.0 * 0.044715 * value * value
    )
    return gelu_value, slope


def far_first(k, n):
    half = n // 2
    return half + ((k + 1) // 2) * (1 - 2 * lax.rem(k, 2))


def loop(n, body):
    def step(k, carry):
        body(k)
        return carry

    lax.fori_loop(0, n, step, 0)


def kernel(
    a_ref, idx_ref, wenc_ref, benc_ref, wdec_ref, bdec_ref, wg_ref, wu_ref, wn_ref, cot_ref,
    out_ref, genc_ref, gencb_ref, gdec_ref, gdecb_ref,
    apad, cpad, X, Y, WE, WD, hit, act, acc, SB, SR, PO, S2, R2, S3, R3, rc16, RC,
    WG, WU, WN, CT, BS, BR, BG, CS, CR, AG, DS, DR, HID, BGT, BUP, BH,
    s_s, s_r, z_s, z_r, t_s, t_r, g_s, g_r,
):
    lat = lax.axis_index("lat")
    tp = lax.axis_index("tp")
    z = lat // 2
    c = lax.rem(lat, 2)
    p = lat // MEM
    m = lax.rem(lat, MEM)
    oc = 1 - c
    sister = lat + 1 - 2 * c

    def copy(src, dst, ss, rs, dl, dt):
        return pltpu.make_async_remote_copy(
            src_ref=src, dst_ref=dst, send_sem=ss, recv_sem=rs, device_id=(dl, dt), device_id_type=MESH
        )

    bar = pltpu.get_barrier_semaphore()

    def hello_z(k):
        d = far_first(k, NZ)
        pl.semaphore_signal(bar, inc=1, device_id=(2 * lax.rem(z + d, NZ) + c, tp), device_id_type=MESH)

    def hello_t(k):
        kk = k + 1
        mm_ = lax.rem(m + kk // NT, MEM)
        tt = lax.rem(tp + lax.rem(kk, NT), NT)
        pl.semaphore_signal(bar, inc=1, device_id=(MEM * p + mm_, tt), device_id_type=MESH)

    loop(NZ - 1, hello_z)
    loop(MEM * NT - 1, hello_t)

    apad[...] = jnp.zeros_like(apad)
    cpad[...] = jnp.zeros_like(cpad)
    apad[:, :, :W] = a_ref[...].reshape(NT, 16, W)
    cpad[:, :, :W] = cot_ref[...].reshape(NT, 16, W)
    X[c, tp, z] = apad[tp]
    WG[m, :W] = wg_ref[...]
    WU[m, :W] = wu_ref[...]
    WN[m] = jnp.zeros((FF, 128), BF)
    WN[m, :, :W] = wn_ref[...]

    def pad_w(g):
        WG[g, W:] = jnp.zeros((128 - W, FF), BF)
        WU[g, W:] = jnp.zeros((128 - W, FF), BF)

    loop(MEM, pad_w)
    CT[m] = cpad[pl.ds(m * TB, TB)]

    pl.semaphore_wait(bar, NZ - 1 + MEM * NT - 1)

    class Gather:
        def __init__(self, buf, n):
            self.buf, self.n = buf, n

        def zcopy(self, d):
            to = lax.rem(z + d, NZ)
            return copy(self.buf.at[c, tp, z], self.buf.at[c, tp, z], z_s.at[self.n, to], z_r.at[self.n, z],
                        2 * to + c, tp)

        def zrecv(self, d):
            fr = lax.rem(z + d, NZ)
            return copy(self.buf.at[c, tp, fr], self.buf.at[c, tp, fr], z_s.at[self.n, fr], z_r.at[self.n, fr],
                        2 * fr + c, tp)

        def tcopy(self, d):
            to = lax.rem(tp + d, NT)
            return copy(self.buf.at[c, tp], self.buf.at[c, tp], t_s.at[self.n, to], t_r.at[self.n, tp], lat, to)

        def trecv(self, d):
            fr = lax.rem(tp + d, NT)
            return copy(self.buf.at[c, fr], self.buf.at[c, fr], t_s.at[self.n, fr], t_r.at[self.n, fr], lat, fr)

        def sis(self, which):
            return copy(self.buf.at[which], self.buf.at[which], s_s.at[self.n], s_r.at[self.n], sister, tp)

        def start_z(self):
            loop(NZ - 1, lambda k: self.zcopy(far_first(k, NZ)).start())

        def z_to_t(self):
            loop(NZ - 1, lambda k: self.zrecv(k + 1).wait_recv())
            loop(NT - 1, lambda k: self.tcopy(k + 1).start())

        def t_to_s(self):
            loop(NT - 1, lambda k: self.trecv(k + 1).wait_recv())
            self.sis(c).start()

        def done(self):
            self.sis(oc).wait_recv()

        def drain(self):
            loop(NZ - 1, lambda k: self.zcopy(k + 1).wait_send())
            loop(NT - 1, lambda k: self.tcopy(k + 1).wait_send())
            self.sis(c).wait_send()

    ga = Gather(X, 0)
    ga.start_z()

    def group_copies(k, own):
        d = k + 1
        mo = lax.rem(m + d, MEM)
        to = MEM * p + mo
        i = m if own else mo
        sem = mo if own else m
        ss, rs = g_s, g_r
        rows = pl.ds(mo * TB, TB)
        src = cpad.at[rows] if own else CT.at[i]
        return [
            copy(src, CT.at[i], ss.at[0, mo], rs.at[0, i], to, tp),
            copy(WN.at[i], WN.at[i], ss.at[1, mo], rs.at[1, i], to, tp),
            copy(WG.at[i, pl.ds(0, W)], WG.at[i, pl.ds(0, W)], ss.at[2, mo], rs.at[2, i], to, tp),
            copy(WU.at[i, pl.ds(0, W)], WU.at[i, pl.ds(0, W)], ss.at[3, mo], rs.at[3, i], to, tp),
        ]

    def start_group(k):
        for cp in group_copies(k, True):
            cp.start()

    loop(MEM - 1, start_group)

    def pad_enc(i):
        blk = wenc_ref[pl.ds(pl.multiple_of(i * W, 16), W), :]
        WE[lax.rem(i, 2), i // 2, :W] = blk
        WE[lax.rem(i, 2), i // 2, W:] = jnp.zeros((128 - W, 128), BF)

    loop(2 * NZ, pad_enc)
    for i in range(2 * NZ):
        WD[i % 2, i // 2] = jnp.zeros((128, 128), BF)
        WD[i % 2, i // 2, :, :W] = wdec_ref[:, i * W:(i + 1) * W]

    cols = (lat * NT + tp) * 128 + lax.broadcasted_iota(jnp.int32, (16, 128), 1)

    def hits(i):
        rows = pl.ds(pl.multiple_of(i * 16, 16), 16)
        ids = idx_ref[rows, :]
        found = jnp.zeros((16, 128), F32)
        for j in range(ids.shape[1]):
            found = jnp.where(ids[:, j:j + 1] == cols, 1.0, found)
        hit[rows, :] = found

    loop(NT, hits)

    ga.z_to_t()

    for k in range(MEM - 1):
        for cp in group_copies(k, False):
            cp.wait_recv()
    bh = mm_nt(CT[0].reshape(RB, 128), WN[0])
    for g in range(1, MEM):
        bh = bh + mm_nt(CT[g].reshape(RB, 128), WN[g])
    BS[...] = bh.reshape(NP, 8, FF)

    def ring(src, dst, n, own_src, send, d):
        q = lax.rem(p + d, NP)
        if send:
            return copy(src.at[q] if own_src else src, dst.at[p], z_s.at[n, q], z_r.at[n, p], MEM * q + m, tp)
        return copy(dst.at[q], dst.at[q], z_s.at[n, q], z_r.at[n, q], MEM * q + m, tp)

    def ring_start(src, dst, n, own_src):
        loop(NP - 1, lambda k: ring(src, dst, n, own_src, True, far_first(k, NP)).start())

    def ring_wait(src, dst, n, own_src):
        loop(NP - 1, lambda k: ring(src, dst, n, own_src, False, k + 1).wait_recv())

    def ring_drain(src, dst, n, own_src):
        loop(NP - 1, lambda k: ring(src, dst, n, own_src, True, k + 1).wait_send())

    BR[p] = BS[p]
    ring_start(BS, BR, 2, True)

    ga.t_to_s()

    def pre_half(h):
        def step(i, s):
            lhs = jnp.concatenate([X[h, :, 2 * i].reshape(256, 128), X[h, :, 2 * i + 1].reshape(256, 128)], axis=1)
            return s + mm(lhs, WE[h, pl.ds(2 * i, 2)].reshape(256, 128))

        acc[...] = lax.fori_loop(0, NZ // 2, step, acc[...])

    acc[...] = jnp.broadcast_to(benc_ref[...], (256, 128))
    pre_half(c)
    ga.done()
    pre_half(oc)
    act[...] = (acc[...] * hit[...]).astype(BF)

    def sis2(h):
        part = pl.ds(h * (NZ // 4), NZ // 4)
        return copy(SB.at[part], SR.at[part], s_s.at[2 + h], s_r.at[2 + h], sister, tp)

    def other(i):
        SB[i] = mm(act[...], WD[oc, i]).astype(BF).reshape(NT, 16, 128)

    for h in range(4):
        loop(NZ // 4, lambda k: other(h * (NZ // 4) + k))
        sis2(h).start()

    def own(i):
        PO[i] = mm(act[...], WD[c, i])

    loop(NZ, own)

    def both(i):
        S2[:, i] = (PO[i] + SR[i].reshape(256, 128).astype(F32)).astype(BF).reshape(NT, 16, 128)

    for h in range(4):
        sis2(h).wait_recv()
        loop(NZ // 4, lambda k: both(h * (NZ // 4) + k))

    def tsum(d, send):
        o = lax.rem(tp + d, NT)
        if send:
            return copy(S2.at[o], R2.at[tp], t_s.at[2, o], t_r.at[2, tp], lat, o)
        return copy(R2.at[o], R2.at[o], t_s.at[2, o], t_r.at[2, o], lat, o)

    loop(NT - 1, lambda k: tsum(k + 1, True).start())
    R2[tp] = S2[tp]

    ring_wait(BS, BR, 2, True)
    BG[p] = jnp.sum(BR[...], axis=0)
    ring_start(BG.at[p], BG, 3, False)

    loop(NT - 1, lambda k: tsum(k + 1, False).wait_recv())

    def tadd(i):
        S3[i] = jnp.sum(R2[:, i].astype(F32), axis=0).astype(BF)

    loop(NZ, tadd)

    def zsum(d, send):
        o = lax.rem(z + d, NZ)
        if send:
            return copy(S3.at[o], R3.at[z], z_s.at[4, o], z_r.at[4, z], 2 * o + c, tp)
        return copy(R3.at[o], R3.at[o], z_s.at[4, o], z_r.at[4, o], 2 * o + c, tp)

    loop(NZ - 1, lambda k: zsum(far_first(k, NZ), True).start())
    R3[z] = S3[z]
    loop(NZ - 1, lambda k: zsum(k + 1, False).wait_recv())
    rc16[...] = (jnp.sum(R3[...].astype(F32), axis=0) + bdec_ref[...]).astype(BF)

    mt = tp // TB
    slot = lax.rem(tp, TB)

    def rcopy(d):
        o = lax.rem(tp + d, NT)
        return copy(rc16, RC.at[m, slot], t_s.at[3, o], t_r.at[3, m * TB + slot], MEM * p + mt, o)

    def rwait(k):
        g = k // TB
        i = lax.rem(k, TB)

        @pl.when(jnp.logical_or(g != m, m * TB + i != tp))
        def _():
            copy(rc16, RC.at[g, i], t_s.at[3, 0], t_r.at[3, k], MEM * p + g, m * TB + i).wait_recv()

    loop(NT - 1, lambda k: rcopy(k + 1).start())

    @pl.when(mt == m)
    def _():
        RC[m, slot] = rc16[...]

    @pl.when(mt != m)
    def _():
        rcopy(0).start()

    loop(MEM * TB, rwait)

    def pairs(i):
        return jnp.concatenate([RC[2 * i].reshape(RB, 128), RC[2 * i + 1].reshape(RB, 128)], axis=1)

    gate = mm(pairs(0), WG[0:2].reshape(256, FF))
    up = mm(pairs(0), WU[0:2].reshape(256, FF))
    for i in range(1, MEM // 2):
        gate = gate + mm(pairs(i), WG[2 * i:2 * i + 2].reshape(256, FF))
        up = up + mm(pairs(i), WU[2 * i:2 * i + 2].reshape(256, FF))
    CS[:, 0:16, :] = jnp.concatenate([gate.reshape(NP, 8, FF), up.reshape(NP, 8, FF)], axis=1).astype(BF)
    ring_start(CS, CR, 5, True)
    CR[p] = CS[p]
    ring_wait(CS, CR, 5, True)
    AG[p] = jnp.sum(CR[...].astype(F32), axis=0).astype(BF)
    ring_start(AG.at[p], AG, 6, False)
    ring_wait(BG.at[p], BG, 3, False)
    ring_wait(AG.at[p], AG, 6, False)

    def cells(i):
        both_ = AG[i].astype(F32)
        gate_, up_ = both_[:8], both_[8:]
        bh_ = BG[i]
        gelu_value, slope = gelu_parts(gate_)
        HID[i] = gelu_value * up_
        BGT[i] = bh_ * up_ * slope
        BUP[i] = bh_ * gelu_value

    loop(NP, cells)
    hidden = HID[...].reshape(RB, FF).astype(BF)
    bgate = BGT[...].reshape(RB, FF).astype(BF)
    bup = BUP[...].reshape(RB, FF).astype(BF)
    for g in range(MEM):
        DS[g, :, 0] = mm(hidden, WN[g]).astype(BF).reshape(TB, 16, 128)
        DS[g, :, 1] = (mm_nt(bgate, WG[g]) + mm_nt(bup, WU[g])).astype(BF).reshape(TB, 16, 128)

    def dcopy(k):
        g = k // TB
        i = lax.rem(k, TB)
        return copy(DS.at[g, i], DR.at[tp], t_s.at[4, k], t_r.at[4, tp], MEM * p + g, m * TB + i)

    def unless_self(k, fn):
        g = k // TB
        i = lax.rem(k, TB)

        @pl.when(jnp.logical_or(g != m, m * TB + i != tp))
        def _():
            fn(k)

    def dwait(d):
        o = lax.rem(tp + d, NT)
        copy(DR.at[o], DR.at[o], t_s.at[4, 0], t_r.at[4, o], MEM * p + mt, o).wait_recv()

    loop(MEM * TB, lambda k: unless_self(k, lambda kk: dcopy(kk).start()))

    @pl.when(mt == m)
    def _():
        DR[tp] = DS[m, slot]

    @pl.when(mt != m)
    def _():
        dwait(0)

    loop(NT - 1, lambda k: dwait(k + 1))
    sums = jnp.sum(DR[...].astype(F32), axis=0)
    recon = rc16[...].astype(F32)
    out_ref[...] = (recon + sums[0]).astype(BF)[:, :W]
    back = cpad[tp].astype(F32) + sums[1] + recon - apad[tp].astype(F32)
    Y[c, tp, z] = back.astype(BF)

    gy = Gather(Y, 1)
    gy.start_z()
    gy.z_to_t()
    gy.t_to_s()

    def back_half(h):
        def step(i, s):
            y = Y[h, :, i].reshape(256, 128)
            gdec_ref[2 * i + h] = mm_tn(act[...], y).astype(BF)
            return s + mm_nt(y, WD[h, i])

        acc[...] = lax.fori_loop(0, NZ, step, acc[...])

    acc[...] = jnp.zeros_like(acc)
    back_half(c)
    gdecb_ref[...] = jnp.sum(Y[c, :, z].reshape(256, 128).astype(F32), axis=0, keepdims=True)
    gy.done()
    back_half(oc)
    bact = (acc[...] * hit[...]).astype(BF)
    gencb_ref[...] = jnp.sum(bact.astype(F32), axis=0, keepdims=True)
    act[...] = bact

    def enc_grad(i):
        x = X[lax.rem(i, 2), :, i // 2].reshape(256, 128)
        genc_ref[pl.ds(pl.multiple_of(i * W, 16), W), :] = mm_tn(x, act[...])[:W].astype(BF)

    loop(2 * NZ, enc_grad)

    ga.drain()
    gy.drain()

    def drain_group(k):
        for cp in group_copies(k, True):
            cp.wait_send()

    loop(MEM - 1, drain_group)
    ring_drain(BS, BR, 2, True)
    ring_drain(BG.at[p], BG, 3, False)
    ring_drain(CS, CR, 5, True)
    ring_drain(AG.at[p], AG, 6, False)
    for h in range(4):
        sis2(h).wait_send()
    loop(NT - 1, lambda k: tsum(k + 1, True).wait_send())
    loop(NZ - 1, lambda k: zsum(k + 1, True).wait_send())
    loop(NT - 1, lambda k: rcopy(k + 1).wait_send())

    @pl.when(mt != m)
    def _():
        rcopy(0).wait_send()

    loop(MEM * TB, lambda k: unless_self(k, lambda kk: dcopy(kk).wait_send()))


def on_device(activations, indices, w_enc, b_enc, w_dec, b_dec, w_gate, w_up, w_down, cotangent):
    vm = pltpu.VMEM
    dma = pltpu.SemaphoreType.DMA
    out, genc, gencb, gdec, gdecb = pl.pallas_call(
        kernel,
        out_shape=(
            jax.ShapeDtypeStruct((16, W), BF),
            jax.ShapeDtypeStruct((2 * NZ * W, 128), BF),
            jax.ShapeDtypeStruct((1, 128), F32),
            jax.ShapeDtypeStruct((2 * NZ, 128, 128), BF),
            jax.ShapeDtypeStruct((1, 128), F32),
        ),
        in_specs=[pl.BlockSpec(memory_space=pltpu.VMEM)] * 10,
        out_specs=[pl.BlockSpec(memory_space=pltpu.VMEM)] * 5,
        scratch_shapes=[
            vm((NT, 16, 128), BF),
            vm((NT, 16, 128), BF),
            vm((2, NT, NZ, 16, 128), BF),
            vm((2, NT, NZ, 16, 128), BF),
            vm((2, NZ, 128, 128), BF),
            vm((2, NZ, 128, 128), BF),
            vm((256, 128), F32),
            vm((256, 128), BF),
            vm((256, 128), F32),
            vm((NZ, NT, 16, 128), BF),
            vm((NZ, NT, 16, 128), BF),
            vm((NZ, 256, 128), F32),
            vm((NT, NZ, 16, 128), BF),
            vm((NT, NZ, 16, 128), BF),
            vm((NZ, 16, 128), BF),
            vm((NZ, 16, 128), BF),
            vm((16, 128), BF),
            vm((MEM, TB, 16, 128), BF),
            vm((MEM, 128, FF), BF),
            vm((MEM, 128, FF), BF),
            vm((MEM, FF, 128), BF),
            vm((MEM, TB, 16, 128), BF),
            vm((NP, 8, FF), F32),
            vm((NP, 8, FF), F32),
            vm((NP, 8, FF), F32),
            vm((NP, 16, FF), BF),
            vm((NP, 16, FF), BF),
            vm((NP, 16, FF), BF),
            vm((MEM, TB, 2, 16, 128), BF),
            vm((NT, 2, 16, 128), BF),
            vm((NP, 8, FF), F32),
            vm((NP, 8, FF), F32),
            vm((NP, 8, FF), F32),
            vm((8, 128), F32),
            dma((6,)), dma((6,)),
            dma((7, NZ)), dma((7, NZ)),
            dma((5, NT)), dma((5, NT)),
            dma((4, MEM)), dma((4, MEM)),
        ],
        compiler_params=pltpu.CompilerParams(
            collective_id=1, has_side_effects=True, vmem_limit_bytes=56 * 2**20
        ),
        cost_estimate=pl.CostEstimate(flops=2 * 10**9, bytes_accessed=6 * 10**6, transcendentals=10**5),
        name="sae_step",
    )(
        activations, indices, w_enc, b_enc.reshape(1, 128), w_dec, jnp.pad(b_dec, (0, 128 - W)).reshape(1, 128),
        w_gate, w_up, w_down, cotangent,
    )
    gdec = gdec[:, :, :W].transpose(1, 0, 2).reshape(128, 2 * NZ * W)
    return out, genc, gencb.reshape(128), gdec, gdecb[0, :W]


def solution(mesh):
    return jax.shard_map(
        on_device,
        mesh=mesh,
        in_specs=(
            P(None, "lat"),
            P(),
            P(None, ("lat", "tp")),
            P(("lat", "tp")),
            P(("lat", "tp"), None),
            P("lat"),
            P("lat", "tp"),
            P("lat", "tp"),
            P("tp", "lat"),
            P(None, "lat"),
        ),
        out_specs=(
            P("tp", "lat"),
            P(None, ("lat", "tp")),
            P(("lat", "tp")),
            P(("lat", "tp"), None),
            P("lat"),
        ),
        check_vma=False,
    )
```

time: 747 us -> 186 us (0.25)
  waiting for transfers between devices: 698 us -> 0 us
  Pallas kernels: 0 us -> 173 us
  matrix products: 21 us -> 0 us
  between operations: 14.9 us -> 0.7 us
    psum x2 -> x0, waiting for transfers between devices: 331 us -> none  [the longest x1 216 us: on_device(): lax.psum((jnp.dot(recon, w_gate, preferred_element_type=jnp.float32), jnp...]
    pallas_call x0 -> x1, Pallas kernels: none -> 173 us  [on_device(): pl.pallas_call(kernel, out_shape=(jax.ShapeDtypeStruct((16, W), BF), jax....]
    all_gather x2 -> x0, waiting for transfers between devices: 146 us -> none  [the longest x1 75.7 us: on_device(): inputs = lax.all_gather(activations, 'lat', axis=1, tiled=True)]
    unnamed x7 -> x0, waiting for transfers between devices: 115 us -> none
    reduce_scatter x1 -> x0, waiting for transfers between devices: 106 us -> none  [on_device(): lax.psum_scatter(partial_value, 'lat', scatter_dimension=1, tiled=True)]
    dot_general x11 -> x0, matrix products: 21 us -> none  [the longest x4 5.84 us: contract_cols(): lax.dot_general(left, right, (((1,), (1,)), ((), ())), preferred_element_...]
  transfers between devices with their start and end apart: 6 -> 0, of which waited for: 6 -> 0; matrix products, arithmetic and copies ran while one was open for 1% -> 0% of each run, Pallas kernels for 0% -> 0%
where the time goes in v1:
time: 186 us; the launch traced here: 185 us
  Pallas kernels  173 us (93%)
  local copies, waits for them, and re-layouts  11.5 us (6%)
    pallas_call x1, Pallas kernels, on_device(): pl.pallas_call(kernel, out_shape=(jax.ShapeDtypeStruct((16, W), BF), jax....  173 us
    unnamed x24, local copies, waits for them, and re-layouts  8.54 us

profile of v1, /device:TPU:1, one launch (start us, length us, event | category | flops | bytes accessed | tf_op | source)
XLA Modules:
  0.0 185.2 jit_solution(5968444386570752876)
XLA Ops:
  0.6 0.0 copy-start.5
  0.6 0.0 copy-start.2
  0.7 0.6 copy-done.5
  1.3 0.0 copy-start.3
  1.3 0.5 pad_bitcast_fusion.bdec_ref
  1.8 0.0 copy-start.1
  1.8 1.6 copy.19.a_ref
  3.4 0.0 copy-done.3
  3.4 0.7 copy.22.cot_ref
  4.1 0.0 copy-done.2
  4.1 0.8 copy.20.idx_ref
  4.9 0.0 copy-done.1
  4.9 0.8 copy.21.wn_ref
  5.7 173.0 %sae_step.1 = (bf16[16,112]{1,0:T(8,128)(2,1)}, bf16[3584,128]{1,0:T(8,128)(2,1)}, f32[1,128]{1,0:T(1,128)}, bf16[32,128,128]{2,1,0:T(8,128)(2,1)}, f32[1,128]{1,0:T(1,128)}) custom-call(bf16[256,112]{1,0:T(8,128)(2,1)} %copy.19.a_ref, s32[256,64]{1,0:T(8,128)} %copy.20.idx_ref, bf16[3584,128]{1,0:T(8,128)(2,1)} %wenc_ref.1, f32[1,128]{1,0:T(1,128)} %bitcast.10, ...), custom_call_target="tpu_custom_call" | custom-call | flops 2000000000 | bytes 6000000 | tf_op jit(solution)/shard_map/sae_step/pallas_call | solution.py:454
  178.8 0.0 copy-start.7
  178.8 0.7 copy-done.7
  179.4 0.5 slice_bitcast_fusion.1
  180.0 1.3 slice_bitcast_fusion
  181.2 0.6 copy.23
  181.9 0.0 copy-start.4
  181.9 0.0 copy-start
  181.9 1.3 copy.24
  183.2 0.0 copy-done.4
  183.2 0.6 copy.28
  183.8 0.0 copy-done
  183.8 0.0 copy-start.6
  183.8 0.9 copy.29
  184.7 0.0 copy-done.6
  184.7 0.5 copy.30
Async XLA Ops:
  0.6 0.7 copy-start.5
  0.6 3.5 %copy-start.2 = (s32[256,64]{0,1:T(8,128)S(1)}, s32[256,64]{0,1:T(8,128)}, u32[]{:S(2)}) copy-start(s32[256,64]{0,1:T(8,128)} %param.11) | copy-start | bytes 196612
  1.3 2.1 %copy-start.3 = (bf16[256,112]{0,1:T(8,128)(2,1)S(1)}, bf16[256,112]{0,1:T(8,128)(2,1)}, u32[]{:S(2)}) copy-start(bf16[256,112]{0,1:T(8,128)(2,1)} %param.19) | copy-start | bytes 172036
  1.8 3.1 %copy-start.1 = (bf16[896,112]{0,1:T(8,128)(2,1)S(1)}, bf16[896,112]{0,1:T(8,128)(2,1)}, u32[]{:S(2)}) copy-start(bf16[896,112]{0,1:T(8,128)(2,1)} %param.18) | copy-start | bytes 602116
  178.8 0.7 copy-start.7
  181.9 1.3 copy-start.4
  181.9 1.9 %copy-start = (bf16[3584,128]{1,0:T(8,128)(2,1)S(1)}, bf16[3584,128]{1,0:T(8,128)(2,1)}, u32[]{:S(2)}) copy-start(bf16[3584,128]{1,0:T(8,128)(2,1)} %get-tuple-element.26) | copy-start | bytes 2752516
  183.8 0.9 copy-start.6

commit v2 on v0

v2 whole, which is shorter than its diff:
```python
import functools

import jax
import jax.numpy as jnp
from jax import lax
from jax.experimental import pallas as pl
from jax.experimental.pallas import tpu as pltpu
from jax.sharding import PartitionSpec as P

MESH = pl.DeviceIdType.MESH
NZ = 16
NT = 16
PAIR = 2
MEM = 2 * PAIR
NP = NZ // PAIR
TB = NT // MEM
RB = 16 * TB
W = 112
FF = 896
NEAR = 9
BF = jnp.bfloat16
F32 = jnp.float32


def mm(a, b):
    return lax.dot_general(a, b, (((1,), (0,)), ((), ())), preferred_element_type=F32)


def mm_nt(a, b):
    return lax.dot_general(a, b, (((1,), (1,)), ((), ())), preferred_element_type=F32)


def gelu_parts(value):
    coeff = 0.7978845608028654
    inner = coeff * (value + 0.044715 * value * value * value)
    tanh_term = jnp.tanh(inner)
    gelu_value = 0.5 * value * (1.0 + tanh_term)
    slope = 0.5 * (1.0 + tanh_term) + 0.5 * value * (1.0 - tanh_term * tanh_term) * coeff * (
        1.0 + 3.0 * 0.044715 * value * value
    )
    return gelu_value, slope


def offset(s):
    return (s + 1) // 2 * (2 * lax.rem(s, 2) - 1)


def mirror(s):
    return jnp.where(jnp.logical_or(s == 0, s == NZ - 1), s, s + 2 * lax.rem(s, 2) - 1)


def slot_of(d):
    d = lax.rem(d + NZ, NZ)
    return jnp.maximum(jnp.where(d <= NZ // 2, 2 * d - 1, 2 * (NZ - d)), 0)


def loop(n, body, start=0):
    def step(k, carry):
        body(k)
        return carry

    lax.fori_loop(start, n, step, 0)


def kernel(
    stop,
    at_ref, idxt_ref, wenc_ref, benc_ref, wdec_ref, bdec_ref, wg_ref, wu_ref, wnt_ref, cott_ref,
    out_ref, genc_ref, gencb_ref, gdec_ref, gdecb_ref,
    apad, cpad, ZA, ZB, X, Y, XT, WE, WD, WDT, hit, hit2, bias2, act, actf, actt, acc, S2, R2, S3, R3, rc16, RC,
    WG, WU, WGT, WUT, WN, CT, BS, BR, BG, CS, CR, AG, DS, DR, HID, BGT, BUP, wdec, wnt,
    s_s, s_r, z_s, z_r, t_s, t_r, g_s, g_r, l_s,
):
    lat = lax.axis_index("lat")
    tp = lax.axis_index("tp")
    z = lat // 2
    c = lax.rem(lat, 2)
    p = lat // MEM
    m = lax.rem(lat, MEM)
    oc = 1 - c
    sister = lat + 1 - 2 * c
    partner = MEM * p + lax.rem(m + 2, MEM)
    drains = []
    comes = {}

    def finish():
        for wait in comes.values():
            wait()
        for wait in drains:
            wait()

    def got(name):
        comes.pop(name)()

    def copy(src, dst, ss, rs, dl, dt):
        return pltpu.make_async_remote_copy(
            src_ref=src, dst_ref=dst, send_sem=ss, recv_sem=rs, device_id=(dl, dt), device_id_type=MESH
        )

    def to_sister(src, dst, n):
        return copy(src, dst, s_s.at[n], s_r.at[n], sister, tp)

    def z_at(s):
        return lax.rem(z + offset(s) + NZ, NZ)

    bar = pltpu.get_barrier_semaphore()

    def hello_z(k):
        pl.semaphore_signal(bar, inc=1, device_id=(2 * z_at(NZ - 1 - k) + c, tp), device_id_type=MESH)

    def hello_t(k):
        kk = k + 1
        mo = lax.rem(m + kk // NT, MEM)
        to = lax.rem(tp + lax.rem(kk, NT), NT)
        pl.semaphore_signal(bar, inc=1, device_id=(MEM * p + mo, to), device_id_type=MESH)

    loop(NZ - 1, hello_z)
    loop(MEM * NT - 1, hello_t)

    top = pl.ds(0, W)
    l_wnt = pltpu.make_async_copy(wnt_ref, wnt.at[top], l_s.at[0])
    l_wg = pltpu.make_async_copy(wg_ref, WG.at[m, top], l_s.at[1])
    l_wu = pltpu.make_async_copy(wu_ref, WU.at[m, top], l_s.at[2])
    l_wd = pltpu.make_async_copy(wdec_ref, wdec, l_s.at[3])

    def l_we(k):
        h = k // NZ
        s = lax.rem(k, NZ)
        rows = pl.ds(pl.multiple_of((2 * z_at(s) + h) * W, 16), W)
        return pltpu.make_async_copy(wenc_ref.at[rows], WE.at[c, s, h, top], l_s.at[4 + k])

    l_wnt.start()
    loop(2 * NZ, lambda k: l_we(k).start())
    l_wd.start()
    l_wg.start()
    l_wu.start()

    fill = jnp.zeros((128 - W, 256), BF)
    apad[...] = jnp.concatenate([at_ref[...], fill], axis=0).T.reshape(NT, 16, 128)
    cpad[...] = jnp.concatenate([cott_ref[...], fill], axis=0).T.reshape(NT, 16, 128)
    ZA[0] = apad[tp]

    def pad_w(g):
        WG[g, W:] = jnp.zeros((128 - W, FF), BF)
        WU[g, W:] = jnp.zeros((128 - W, FF), BF)

    def pad_e(k):
        WE[c, k // 2, lax.rem(k, 2), W:] = jnp.zeros((128 - W, 128), BF)

    loop(MEM, pad_w)
    loop(2 * NZ, pad_e)
    wnt[W:] = jnp.zeros((128 - W, FF), BF)
    CT[m] = cpad[pl.ds(m * TB, TB)]
    l_wnt.wait()
    WN[m] = wnt[...].T

    pl.semaphore_wait(bar, NZ - 1 + MEM * NT - 1)
    if stop == 0:
        loop(2 * NZ, lambda k: l_we(k).wait())
        l_wg.wait()
        l_wu.wait()
        l_wd.wait()
        return finish()

    ht = tp // 8
    jt = lax.rem(tp, 8)

    class Gather:
        def __init__(self, zb, buf, n):
            self.zb, self.buf, self.n = zb, buf, n

        def z_out(self, s):
            r = mirror(s)
            return copy(self.zb.at[0], self.zb.at[r], z_s.at[self.n, s], z_r.at[self.n, r], 2 * z_at(s) + c, tp)

        def z_in(self, s):
            return copy(self.zb.at[s], self.zb.at[s], z_s.at[self.n, s], z_r.at[self.n, s], 2 * z_at(s) + c, tp)

        def rows(self, w):
            return pl.ds(0, NEAR) if w == 0 else pl.ds(NEAR, NZ - NEAR)

        def t_out(self, w, d):
            to = lax.rem(tp + d, NT)
            sem = 2 * self.n + w
            return copy(self.zb.at[self.rows(w)], self.buf.at[ht, jt, c, self.rows(w)],
                        t_s.at[sem, to], t_r.at[sem, c * 8 + jt], 2 * z + ht, to)

        def t_in(self, w, k):
            dst = self.buf.at[c, lax.rem(k, 8), k // 8, self.rows(w)]
            sem = 2 * self.n + w
            return copy(dst, dst, t_s.at[sem, 0], t_r.at[sem, k], 2 * z + k // 8, c * 8 + lax.rem(k, 8))

        def sis(self, which, w):
            part = self.buf.at[which, :, :, self.rows(w)]
            return to_sister(part, part, 2 * self.n + w)

        def start(self):
            loop(NZ - 1, lambda k: self.z_out(NZ - 1 - k).start())
            drains.append(lambda: loop(NZ, lambda s: self.z_out(s).wait_send(), 1))
            comes["z0"] = lambda: loop(NEAR, lambda s: self.z_in(s).wait_recv(), 1)
            comes["z1"] = lambda: loop(NZ, lambda s: self.z_in(s).wait_recv(), NEAR)

        def forward(self, w):
            got("z%d" % w)
            loop(NT, lambda d: self.t_out(w, d).start(), 1)

            @pl.when(ht != c)
            def _():
                self.t_out(w, 0).start()

            @pl.when(ht == c)
            def _():
                self.buf[c, jt, c, self.rows(w)] = self.zb[self.rows(w)]

            def drain():
                loop(NT, lambda d: self.t_out(w, d).wait_send(), 1)

                @pl.when(ht != c)
                def _():
                    self.t_out(w, 0).wait_send()

            def come(k):
                @pl.when(jnp.logical_or(k // 8 != c, c * 8 + lax.rem(k, 8) != tp))
                def _():
                    self.t_in(w, k).wait_recv()

            drains.append(drain)
            comes["t%d" % w] = lambda: loop(NT, come)

        def swap(self, w):
            self.sis(c, w).start()
            drains.append(lambda: self.sis(c, w).wait_send())
            comes["sis%d%d" % (self.n, w)] = lambda: self.sis(oc, w).wait_recv()

    ga = Gather(ZA, X, 0)
    ga.start()

    def weight(a, i):
        return [WN.at[i], WG.at[i, top], WU.at[i, top]][a]

    def share(a, i, to):
        return copy(weight(a, i), weight(a, i), g_s.at[a, i, 0 if to is sister else 1], g_r.at[a, i], to, tp)

    slot_p = lax.rem(m + 2, MEM)
    slot_s = m + 1 - 2 * c
    slot_sp = lax.rem(slot_s + 2, MEM)

    def share_out(a):
        share(a, m, sister).start()
        share(a, m, partner).start()
        drains.append(lambda: [share(a, m, sister).wait_send(), share(a, m, partner).wait_send()])
        comes["sis w%d" % a] = lambda: share(a, slot_s, sister).wait_recv()
        comes["chip w%d" % a] = lambda: share(a, slot_p, partner).wait_recv()

    def share_on(a):
        got("chip w%d" % a)
        share(a, slot_p, sister).start()
        drains.append(lambda: share(a, slot_p, sister).wait_send())
        comes["last w%d" % a] = lambda: share(a, slot_sp, sister).wait_recv()

    def cot_out(d):
        mo = lax.rem(m + d, MEM)
        return copy(cpad.at[pl.ds(mo * TB, TB)], CT.at[m], g_s.at[3, mo, 0], g_r.at[3, m], MEM * p + mo, tp)

    def cot_in(d):
        mo = lax.rem(m + d, MEM)
        return copy(CT.at[mo], CT.at[mo], g_s.at[3, mo, 0], g_r.at[3, mo], MEM * p + mo, tp)

    loop(MEM, lambda d: cot_out(d).start(), 1)
    drains.append(lambda: loop(MEM, lambda d: cot_out(d).wait_send(), 1))
    comes["cot"] = lambda: loop(MEM, lambda d: cot_in(d).wait_recv(), 1)
    share_out(0)

    ids_col = (lat * NT + tp) * 128 + lax.broadcasted_iota(jnp.int32, (128, 256), 0)

    def one_hit(j, found):
        return jnp.where(idxt_ref[pl.ds(j, 1), :] == ids_col, 1.0, found)

    hit[...] = lax.fori_loop(0, idxt_ref.shape[0], one_hit, jnp.zeros((128, 256), F32), unroll=8).T
    other_rows = pl.ds(pl.multiple_of(oc * 128, 128), 128)
    own_rows = pl.ds(pl.multiple_of(c * 128, 128), 128)
    hit2[c] = hit[own_rows, :]

    def hit_swap():
        return to_sister(hit.at[other_rows], hit2.at[c], 4)

    hit_swap().start()
    drains.append(lambda: hit_swap().wait_send())
    bias2[c] = jnp.broadcast_to(benc_ref[...], (8, 128))

    def bias_swap(i):
        return to_sister(bias2.at[i], bias2.at[i], 8)

    bias_swap(c).start()
    drains.append(lambda: bias_swap(c).wait_send())
    comes["bias"] = lambda: bias_swap(oc).wait_recv()
    comes["hit"] = lambda: to_sister(hit2.at[oc], hit2.at[oc], 4).wait_recv()

    loop(2 * NZ, lambda k: l_we(k).wait())

    def enc_swap(i):
        return to_sister(WE.at[i], WE.at[i], 5)

    enc_swap(c).start()
    drains.append(lambda: enc_swap(c).wait_send())
    comes["enc"] = lambda: enc_swap(oc).wait_recv()

    ga.forward(0)

    l_wd.wait()

    def dec_block(i):
        blk = jnp.concatenate([wdec[:, i * W:(i + 1) * W], jnp.zeros((128, 128 - W), BF)], axis=1)
        s = slot_of(i // 2 - z)
        WD[c, i % 2, s] = blk
        WDT[s, i % 2] = blk.T

    for i in range(NZ):
        dec_block(i)
    ga.forward(1)
    for i in range(NZ, 2 * NZ):
        dec_block(i)

    def dec_swap(i):
        return to_sister(WD.at[i], WD.at[i], 6)

    dec_swap(c).start()
    drains.append(lambda: dec_swap(c).wait_send())
    comes["dec"] = lambda: dec_swap(oc).wait_recv()
    l_wg.wait()
    l_wu.wait()
    share_out(1)
    share_out(2)
    share_on(0)
    if stop == 1:
        return finish()

    def ring(src, dst, n, own_src, send, d):
        q = lax.rem(p + d, NP)
        if send:
            return copy(src.at[q] if own_src else src, dst.at[p], z_s.at[n, q], z_r.at[n, p], MEM * q + m, tp)
        return copy(dst.at[q], dst.at[q], z_s.at[n, q], z_r.at[n, q], MEM * q + m, tp)

    def far(k):
        return NP // 2 + (k + 1) // 2 * (1 - 2 * lax.rem(k, 2))

    def ring_start(src, dst, n, own_src, name):
        loop(NP - 1, lambda k: ring(src, dst, n, own_src, True, far(k)).start())
        drains.append(lambda: loop(NP, lambda d: ring(src, dst, n, own_src, True, d).wait_send(), 1))
        comes[name] = lambda: loop(NP, lambda d: ring(src, dst, n, own_src, False, d).wait_recv(), 1)

    got("cot")
    got("sis w0")
    got("last w0")
    bh = mm_nt(CT[0].reshape(RB, 128), WN[0])
    for g in range(1, MEM):
        bh = bh + mm_nt(CT[g].reshape(RB, 128), WN[g])
    BS[...] = bh.reshape(NP, 8, FF)
    BR[p] = BS[p]
    ring_start(BS, BR, 2, True, "bh sum")
    if stop == 2:
        return finish()

    def pre_part(start, lo, hi):
        pre = start
        for i in range(lo, hi):
            lhs = jnp.concatenate([X[c, :, 0, i].reshape(128, 128), X[c, :, 1, i].reshape(128, 128)], axis=1)
            rhs = jnp.concatenate([WE[0, i].reshape(256, 128), WE[1, i].reshape(256, 128)], axis=1)
            pre = pre + mm(lhs, rhs)
        return pre

    got("bias")
    got("enc")
    got("hit")
    got("t0")
    ga.swap(0)
    pre = pre_part(jnp.concatenate([bias2[0, 0:1], bias2[1, 0:1]], axis=1), 0, NEAR)
    got("t1")
    ga.swap(1)
    pre = pre_part(pre, NEAR, NZ)
    act[...] = (pre * jnp.concatenate([hit2[0], hit2[1]], axis=1)).astype(BF)
    if stop == 3:
        return finish()

    got("dec")
    half = NZ // 2

    def tsum_out(w, k):
        rows = pl.ds(w * half, half)
        return copy(S2.at[lax.rem(k, 8), k // 8, rows], R2.at[tp, rows], t_s.at[4 + w, k], t_r.at[4 + w, tp],
                    2 * z + k // 8, c * 8 + lax.rem(k, 8))

    def tsum_in(w, o):
        rows = pl.ds(w * half, half)
        return copy(R2.at[o, rows], R2.at[o, rows], t_s.at[4 + w, o], t_r.at[4 + w, o], 2 * z + ht, o)

    def unless_me(k, fn):
        @pl.when(jnp.logical_or(k // 8 != c, c * 8 + lax.rem(k, 8) != tp))
        def _():
            fn()

    def tsum_come(w):
        loop(NT, lambda d: tsum_in(w, lax.rem(tp + d, NT)).wait_recv(), 1)

        @pl.when(ht != c)
        def _():
            tsum_in(w, tp).wait_recv()

    for w in (1, 0):
        for i in range(w * half, (w + 1) * half):
            rhs = jnp.concatenate([jnp.concatenate([WD[0, e, i], WD[1, e, i]], axis=0) for e in (0, 1)], axis=1)
            both = mm(act[...], rhs).astype(BF)
            S2[:, 0, i] = both[:, :128].reshape(8, 16, 128)
            S2[:, 1, i] = both[:, 128:].reshape(8, 16, 128)
        loop(NT, lambda k: unless_me(k, lambda: tsum_out(w, k).start()))

        @pl.when(ht == c)
        def _():
            rows = pl.ds(w * half, half)
            R2[tp, rows] = S2[jt, c, rows]

        drains.append(functools.partial(
            lambda w: loop(NT, lambda k: unless_me(k, lambda: tsum_out(w, k).wait_send())), w))
        comes["ts%d" % w] = functools.partial(tsum_come, w)
    if stop == 4:
        return finish()

    actf[c] = act[:, pl.ds(pl.multiple_of(c * 128, 128), 128)]

    def act_swap():
        return to_sister(act.at[:, pl.ds(pl.multiple_of(oc * 128, 128), 128)], actf.at[c], 7)

    act_swap().start()
    drains.append(lambda: act_swap().wait_send())
    comes["act"] = lambda: to_sister(actf.at[oc], actf.at[oc], 7).wait_recv()

    share_on(1)
    share_on(2)
    got("sis00")
    got("sis01")
    got("bh sum")
    BG[p] = jnp.sum(BR[...], axis=0)
    ring_start(BG.at[p], BG, 3, False, "bh")

    def z_out(s):
        r = mirror(s)
        return copy(S3.at[s], R3.at[r], z_s.at[4, s], z_r.at[4, r], 2 * z_at(s) + c, tp)

    def z_in(s):
        return copy(R3.at[s], R3.at[s], z_s.at[4, s], z_r.at[4, s], 2 * z_at(s) + c, tp)

    def tadd(s):
        S3[s] = jnp.sum(R2[:, s].astype(F32), axis=0).astype(BF)

    def far_sum(k):
        tadd(NZ - 1 - k)
        z_out(NZ - 1 - k).start()

    got("ts1")
    loop(half, far_sum)
    got("ts0")
    loop(half - 1, lambda k: far_sum(k + half))
    tadd(0)
    R3[0] = S3[0]
    drains.append(lambda: loop(NZ, lambda s: z_out(s).wait_send(), 1))
    comes["z sum"] = lambda: loop(NZ, lambda s: z_in(s).wait_recv(), 1)
    if stop == 5:
        return finish()
    for a in (1, 2):
        got("sis w%d" % a)
        got("last w%d" % a)
    for g in range(MEM):
        WGT[g] = WG[g].T
        WUT[g] = WU[g].T
    got("z sum")
    bias = jnp.concatenate([bdec_ref[...], jnp.zeros((1, 128 - W), F32)], axis=1)
    rc16[...] = (jnp.sum(R3[...].astype(F32), axis=0) + bias).astype(BF)
    if stop == 6:
        return finish()

    mt = tp // TB
    slot = lax.rem(tp, TB)

    def rcopy(d):
        o = lax.rem(tp + d, NT)
        return copy(rc16, RC.at[m, slot], t_s.at[6, o], t_r.at[6, m * TB + slot], MEM * p + mt, o)

    def unless_self(k, fn):
        g = k // TB
        i = lax.rem(k, TB)

        @pl.when(jnp.logical_or(g != m, m * TB + i != tp))
        def _():
            fn(k)

    def rwait(k):
        g = k // TB
        i = lax.rem(k, TB)
        copy(rc16, RC.at[g, i], t_s.at[6, 0], t_r.at[6, k], MEM * p + g, m * TB + i).wait_recv()

    loop(NT, lambda d: rcopy(d).start(), 1)

    @pl.when(mt == m)
    def _():
        RC[m, slot] = rc16[...]

    @pl.when(mt != m)
    def _():
        rcopy(0).start()

    def rdrain():
        loop(NT, lambda d: rcopy(d).wait_send(), 1)

        @pl.when(mt != m)
        def _():
            rcopy(0).wait_send()

    drains.append(rdrain)
    loop(MEM * TB, lambda k: unless_self(k, rwait))
    if stop == 7:
        return finish()

    def pairs(i):
        return jnp.concatenate([RC[2 * i].reshape(RB, 128), RC[2 * i + 1].reshape(RB, 128)], axis=1)

    gate = mm(pairs(0), WG[0:2].reshape(256, FF))
    up = mm(pairs(0), WU[0:2].reshape(256, FF))
    for i in range(1, MEM // 2):
        gate = gate + mm(pairs(i), WG[2 * i:2 * i + 2].reshape(256, FF))
        up = up + mm(pairs(i), WU[2 * i:2 * i + 2].reshape(256, FF))
    CS[...] = jnp.concatenate([gate.reshape(NP, 8, FF), up.reshape(NP, 8, FF)], axis=1).astype(BF)
    ring_start(CS, CR, 5, True, "gate sum")
    CR[p] = CS[p]
    for h in range(2):
        for i in range(NZ):
            XT[h, i] = X[:, :, h, i].reshape(256, 128).T
    got("act")
    actt[...] = actf[...].reshape(256, 128).T
    if stop == 8:
        return finish()
    got("gate sum")
    AG[p] = jnp.sum(CR[...].astype(F32), axis=0).astype(BF)
    ring_start(AG.at[p], AG, 6, False, "gate")
    got("bh")
    got("gate")
    if stop == 9:
        return finish()

    def cells(i):
        both_ = AG[i].astype(F32)
        gate_, up_ = both_[:8], both_[8:]
        bh_ = BG[i]
        gelu_value, slope = gelu_parts(gate_)
        HID[i] = gelu_value * up_
        BGT[i] = bh_ * up_ * slope
        BUP[i] = bh_ * gelu_value

    loop(NP, cells)
    hidden = HID[...].reshape(RB, FF).astype(BF)
    bgate = BGT[...].reshape(RB, FF).astype(BF)
    bup = BUP[...].reshape(RB, FF).astype(BF)
    for g in range(MEM):
        DS[g, :, 0] = mm(hidden, WN[g]).astype(BF).reshape(TB, 16, 128)
        DS[g, :, 1] = (mm(bgate, WGT[g]) + mm(bup, WUT[g])).astype(BF).reshape(TB, 16, 128)
    if stop == 10:
        return finish()

    def dcopy(k):
        g = k // TB
        i = lax.rem(k, TB)
        return copy(DS.at[g, i], DR.at[tp], t_s.at[7, k], t_r.at[7, tp], MEM * p + g, m * TB + i)

    def dwait(d):
        o = lax.rem(tp + d, NT)
        copy(DR.at[o], DR.at[o], t_s.at[7, 0], t_r.at[7, o], MEM * p + mt, o).wait_recv()

    loop(MEM * TB, lambda k: unless_self(k, lambda kk: dcopy(kk).start()))
    drains.append(lambda: loop(MEM * TB, lambda k: unless_self(k, lambda kk: dcopy(kk).wait_send())))

    @pl.when(mt == m)
    def _():
        DR[tp] = DS[m, slot]

    @pl.when(mt != m)
    def _():
        dwait(0)

    loop(NT, dwait, 1)
    sums = jnp.sum(DR[...].astype(F32), axis=0)
    recon = rc16[...].astype(F32)
    back = cpad[tp].astype(F32) + sums[1] + recon - apad[tp].astype(F32)
    ZB[0] = back.astype(BF)
    if stop == 11:
        return finish()

    gy = Gather(ZB, Y, 1)
    gy.start()
    out_ref[...] = (recon + sums[0]).astype(BF)[:, :W]
    gy.forward(0)
    if stop == 12:
        return finish()
    gy.forward(1)
    if stop == 13:
        return finish()

    acc[...] = jnp.zeros_like(acc)

    def back_part(h, lo, hi):
        s = acc[h]
        for i in range(lo, hi):
            lhs = jnp.concatenate([Y[h, :, 0, i].reshape(128, 128), Y[h, :, 1, i].reshape(128, 128)], axis=1)
            s = s + mm(lhs, WDT[i].reshape(256, 128))
        acc[h] = s

    got("t0")
    gy.swap(0)
    back_part(c, 0, NEAR)
    got("t1")
    gy.swap(1)
    back_part(c, NEAR, NZ)
    got("sis10")
    back_part(oc, 0, NEAR)
    got("sis11")
    back_part(oc, NEAR, NZ)
    if stop == 14:
        return finish()
    bact = (acc[...].reshape(256, 128) * hit[...]).astype(BF)
    gencb_ref[...] = jnp.sum(bact.astype(F32), axis=0)
    gdecb_ref[...] = jnp.sum(Y[:, :, c, 0].reshape(256, 128).astype(F32), axis=0)[:W]
    actf[...] = bact.reshape(2, 128, 128)

    def enc_grad(k):
        h = k // NZ
        s = lax.rem(k, NZ)
        rows = pl.ds(pl.multiple_of((2 * z_at(s) + h) * W, 16), W)
        genc_ref[rows, :] = mm(XT[h, s], actf[...].reshape(256, 128))[:W].astype(BF)

    lax.fori_loop(0, 2 * NZ, lambda k, n: (enc_grad(k), n)[1], 0, unroll=4)
    for i in range(2 * NZ):
        y = Y[:, :, i % 2, slot_of(i // 2 - z)].reshape(256, 128)
        gdec_ref[:, i * W:(i + 1) * W] = mm(actt[...], y)[:, :W].astype(BF)
    finish()


def step(activations, indices, w_enc, b_enc, w_dec, b_dec, w_gate, w_up, w_down, cotangent, stop=99, cid=1):
    vm = pltpu.VMEM
    dma = pltpu.SemaphoreType.DMA
    inside = pl.BlockSpec(memory_space=pltpu.VMEM)
    outside = pl.BlockSpec(memory_space=pl.ANY)
    return pl.pallas_call(
        functools.partial(kernel, stop),
        out_shape=(
            jax.ShapeDtypeStruct((16, W), BF),
            jax.ShapeDtypeStruct((2 * NZ * W, 128), BF),
            jax.ShapeDtypeStruct((128,), F32),
            jax.ShapeDtypeStruct((128, 2 * NZ * W), BF),
            jax.ShapeDtypeStruct((W,), F32),
        ),
        in_specs=[inside, inside, outside, inside, outside, inside, outside, outside, outside, inside],
        out_specs=[inside] * 5,
        scratch_shapes=[
            vm((NT, 16, 128), BF),
            vm((NT, 16, 128), BF),
            vm((NZ, 16, 128), BF),
            vm((NZ, 16, 128), BF),
            vm((2, 8, 2, NZ, 16, 128), BF),
            vm((2, 8, 2, NZ, 16, 128), BF),
            vm((2, NZ, 128, 256), BF),
            vm((2, NZ, 2, 128, 128), BF),
            vm((2, 2, NZ, 128, 128), BF),
            vm((NZ, 2, 128, 128), BF),
            vm((256, 128), F32),
            vm((2, 128, 128), F32),
            vm((2, 8, 128), F32),
            vm((128, 256), BF),
            vm((2, 128, 128), BF),
            vm((128, 256), BF),
            vm((2, 128, 128), F32),
            vm((8, 2, NZ, 16, 128), BF),
            vm((NT, NZ, 16, 128), BF),
            vm((NZ, 16, 128), BF),
            vm((NZ, 16, 128), BF),
            vm((16, 128), BF),
            vm((MEM, TB, 16, 128), BF),
            vm((MEM, 128, FF), BF),
            vm((MEM, 128, FF), BF),
            vm((MEM, FF, 128), BF),
            vm((MEM, FF, 128), BF),
            vm((MEM, FF, 128), BF),
            vm((MEM, TB, 16, 128), BF),
            vm((NP, 8, FF), F32),
            vm((NP, 8, FF), F32),
            vm((NP, 8, FF), F32),
            vm((NP, 16, FF), BF),
            vm((NP, 16, FF), BF),
            vm((NP, 16, FF), BF),
            vm((MEM, TB, 2, 16, 128), BF),
            vm((NT, 2, 16, 128), BF),
            vm((NP, 8, FF), F32),
            vm((NP, 8, FF), F32),
            vm((NP, 8, FF), F32),
            vm((128, 2 * NZ * W), BF),
            vm((128, FF), BF),
            dma((9,)), dma((9,)),
            dma((7, NZ)), dma((7, NZ)),
            dma((8, NT)), dma((8, NT)),
            dma((4, MEM, 2)), dma((4, MEM)),
            dma((4 + 2 * NZ,)),
        ],
        compiler_params=pltpu.CompilerParams(
            collective_id=cid, has_side_effects=True, vmem_limit_bytes=56 * 2**20
        ),
        cost_estimate=pl.CostEstimate(flops=2 * 10**9, bytes_accessed=6 * 10**6, transcendentals=10**5),
        name="sae_step",
    )(
        activations.T, indices.T, w_enc, b_enc.reshape(1, 128), w_dec, b_dec.reshape(1, W),
        w_gate, w_up, w_down.T, cotangent.T,
    )


def solution(mesh):
    return jax.shard_map(
        step,
        mesh=mesh,
        in_specs=(
            P(None, "lat"),
            P(),
            P(None, ("lat", "tp")),
            P(("lat", "tp")),
            P(("lat", "tp"), None),
            P("lat"),
            P("lat", "tp"),
            P("lat", "tp"),
            P("tp", "lat"),
            P(None, "lat"),
        ),
        out_specs=(
            P("tp", "lat"),
            P(None, ("lat", "tp")),
            P(("lat", "tp")),
            P(("lat", "tp"), None),
            P("lat"),
        ),
        check_vma=False,
    )
```

time: 747 us -> 140 us (0.19)
  waiting for transfers between devices: 698 us -> 0 us
  Pallas kernels: 0 us -> 133 us
  matrix products: 21 us -> 0 us
  between operations: 14.9 us -> 0.66 us
    psum x2 -> x0, waiting for transfers between devices: 331 us -> none  [the longest x1 216 us: on_device(): lax.psum((jnp.dot(recon, w_gate, preferred_element_type=jnp.float32), jnp...]
    all_gather x2 -> x0, waiting for transfers between devices: 146 us -> none  [the longest x1 75.7 us: on_device(): inputs = lax.all_gather(activations, 'lat', axis=1, tiled=True)]
    pallas_call x0 -> x1, Pallas kernels: none -> 133 us  [step(): pl.pallas_call(functools.partial(kernel, stop), out_shape=(jax.ShapeDtype...]
    unnamed x7 -> x0, waiting for transfers between devices: 115 us -> none
    reduce_scatter x1 -> x0, waiting for transfers between devices: 106 us -> none  [on_device(): lax.psum_scatter(partial_value, 'lat', scatter_dimension=1, tiled=True)]
    dot_general x11 -> x0, matrix products: 21 us -> none  [the longest x4 5.84 us: contract_cols(): lax.dot_general(left, right, (((1,), (1,)), ((), ())), preferred_element_...]
  transfers between devices with their start and end apart: 6 -> 0, of which waited for: 6 -> 0; matrix products, arithmetic and copies ran while one was open for 1% -> 0% of each run, Pallas kernels for 0% -> 0%
where the time goes in v2:
time: 140 us; the launch traced here: 139 us
  Pallas kernels  133 us (95%)
  local copies, waits for them, and re-layouts  5.46 us (4%)
    pallas_call x1, Pallas kernels, step(): pl.pallas_call(functools.partial(kernel, stop), out_shape=(jax.ShapeDtype...  133 us
    unnamed x13, local copies, waits for them, and re-layouts  5.46 us

profile of v2, /device:TPU:1, one launch (start us, length us, event | category | flops | bytes accessed | tf_op | source)
XLA Modules:
  0.0 139.4 jit_solution(11213623908916976306)
XLA Ops:
  0.6 133.3 %sae_step.1 = (bf16[16,112]{1,0:T(8,128)(2,1)}, bf16[3584,128]{1,0:T(8,128)(2,1)}, f32[128]{0:T(128)}, bf16[128,3584]{1,0:T(8,128)(2,1)}, f32[112]{0:T(128)}) custom-call(bf16[112,256]{1,0:T(8,128)(2,1)} %bitcast.8, s32[64,256]{1,0:T(8,128)} %bitcast.7, bf16[3584,128]{1,0:T(8,128)(2,1)} %wenc_ref.1, f32[1,128]{1,0:T(1,128)} %bitcast.10, ...), custom_call_target="tpu_custom_call" | custom-call | flops 2000000000 | bytes 6000000 | tf_op jit(solution)/shard_map/sae_step/pallas_call | solution.py:649
  133.9 0.0 copy-start.1
  133.9 0.7 copy-done.1
  134.6 0.6 copy.20
  135.2 0.0 copy-start.3
  135.2 0.0 copy-start
  135.2 2.2 %copy.21 = bf16[3584,128]{1,0:T(8,128)(2,1)} copy(bf16[3584,128]{1,0:T(8,128)(2,1)} %get-tuple-element.11) | data formatting | bytes 1835008
  137.5 0.0 copy-done.3
  137.5 0.5 copy.22
  138.0 0.0 copy-done
  138.0 0.0 copy-start.2
  138.0 0.9 copy.23
  138.9 0.0 copy-done.2
  138.9 0.5 copy.24
Async XLA Ops:
  133.9 0.7 copy-start.1
  135.2 2.2 %copy-start.3 = (f32[128]{0:T(128)S(1)}, f32[128]{0:T(128)}, u32[]{:S(2)}) copy-start(f32[128]{0:T(128)} %get-tuple-element.12) | copy-start | bytes 1540
  135.2 2.8 %copy-start = (bf16[128,3584]{1,0:T(8,128)(2,1)S(1)}, bf16[128,3584]{1,0:T(8,128)(2,1)}, u32[]{:S(2)}) copy-start(bf16[128,3584]{1,0:T(8,128)(2,1)} %get-tuple-element.13) | copy-start | bytes 2752516
  138.0 0.9 copy-start.2

commit v3 on v2

--- a/solution.py
+++ b/solution.py
@@ -42,11 +42,16 @@
 
 
 def offset(s):
-    return (s + 1) // 2 * (2 * lax.rem(s, 2) - 1)
+    return (s + 1) // 2 * (2 * (s % 2) - 1)
 
 
 def mirror(s):
-    return jnp.where(jnp.logical_or(s == 0, s == NZ - 1), s, s + 2 * lax.rem(s, 2) - 1)
+    return s if s in (0, NZ - 1) else s + 2 * (s % 2) - 1
+
+
+def plus(v, d, n):
+    v = v + d
+    return v if d == 0 else jnp.where(v >= n, v - n, v) if d > 0 else jnp.where(v < 0, v + n, v)
 
 
 def slot_of(d):
@@ -54,12 +59,18 @@
     return jnp.maximum(jnp.where(d <= NZ // 2, 2 * d - 1, 2 * (NZ - d)), 0)
 
 
+def folded(v):
+    rest = jnp.concatenate([v[..., 512:], jnp.zeros(v.shape[:-1] + (128,), v.dtype)], axis=-1)
+    return jnp.concatenate([v[..., :512], rest], axis=-2)
+
+
+def unfolded(v):
+    return jnp.concatenate([v[..., :8, :], v[..., 8:, :384]], axis=-1)
+
+
 def loop(n, body, start=0):
-    def step(k, carry):
+    for k in range(start, n):
         body(k)
-        return carry
-
-    lax.fori_loop(start, n, step, 0)
 
 
 def kernel(
@@ -67,7 +78,7 @@
     at_ref, idxt_ref, wenc_ref, benc_ref, wdec_ref, bdec_ref, wg_ref, wu_ref, wnt_ref, cott_ref,
     out_ref, genc_ref, gencb_ref, gdec_ref, gdecb_ref,
     apad, cpad, ZA, ZB, X, Y, XT, WE, WD, WDT, hit, hit2, bias2, act, actf, actt, acc, S2, R2, S3, R3, rc16, RC,
-    WG, WU, WGT, WUT, WN, CT, BS, BR, BG, CS, CR, AG, DS, DR, HID, BGT, BUP, wdec, wnt,
+    WG, WU, WGT, WUT, WN, CT, BS, BR, BG, CS, CR, AG, DS, DR, DT, RT, HID, BGT, BUP, wdec, wnt,
     s_s, s_r, z_s, z_r, t_s, t_r, g_s, g_r, l_s,
 ):
     lat = lax.axis_index("lat")
@@ -77,6 +88,10 @@
     p = lat // MEM
     m = lax.rem(lat, MEM)
     oc = 1 - c
+    ht = tp // 8
+    jt = lax.rem(tp, 8)
+    mt = tp // TB
+    slot = lax.rem(tp, TB)
     sister = lat + 1 - 2 * c
     partner = MEM * p + lax.rem(m + 2, MEM)
     drains = []
@@ -100,7 +115,7 @@
         return copy(src, dst, s_s.at[n], s_r.at[n], sister, tp)
 
     def z_at(s):
-        return lax.rem(z + offset(s) + NZ, NZ)
+        return plus(z, offset(s), NZ)
 
     bar = pltpu.get_barrier_semaphore()
 
@@ -109,8 +124,8 @@
 
     def hello_t(k):
         kk = k + 1
-        mo = lax.rem(m + kk // NT, MEM)
-        to = lax.rem(tp + lax.rem(kk, NT), NT)
+        mo = plus(m, kk // NT, MEM)
+        to = plus(tp, kk % NT, NT)
         pl.semaphore_signal(bar, inc=1, device_id=(MEM * p + mo, to), device_id_type=MESH)
 
     loop(NZ - 1, hello_z)
@@ -124,7 +139,7 @@
 
     def l_we(k):
         h = k // NZ
-        s = lax.rem(k, NZ)
+        s = k % NZ
         rows = pl.ds(pl.multiple_of((2 * z_at(s) + h) * W, 16), W)
         return pltpu.make_async_copy(wenc_ref.at[rows], WE.at[c, s, h, top], l_s.at[4 + k])
 
@@ -144,7 +159,7 @@
         WU[g, W:] = jnp.zeros((128 - W, FF), BF)
 
     def pad_e(k):
-        WE[c, k // 2, lax.rem(k, 2), W:] = jnp.zeros((128 - W, 128), BF)
+        WE[c, k // 2, k % 2, W:] = jnp.zeros((128 - W, 128), BF)
 
     loop(MEM, pad_w)
     loop(2 * NZ, pad_e)
@@ -161,9 +176,6 @@
         l_wd.wait()
         return finish()
 
-    ht = tp // 8
-    jt = lax.rem(tp, 8)
-
     class Gather:
         def __init__(self, zb, buf, n):
             self.zb, self.buf, self.n = zb, buf, n
@@ -179,15 +191,17 @@
             return pl.ds(0, NEAR) if w == 0 else pl.ds(NEAR, NZ - NEAR)
 
         def t_out(self, w, d):
-            to = lax.rem(tp + d, NT)
+            to = plus(tp, d, NT)
             sem = 2 * self.n + w
             return copy(self.zb.at[self.rows(w)], self.buf.at[ht, jt, c, self.rows(w)],
                         t_s.at[sem, to], t_r.at[sem, c * 8 + jt], 2 * z + ht, to)
 
         def t_in(self, w, k):
-            dst = self.buf.at[c, lax.rem(k, 8), k // 8, self.rows(w)]
+            e = plus(c, k // 8, 2)
+            j = plus(jt, k % 8, 8)
+            dst = self.buf.at[c, j, e, self.rows(w)]
             sem = 2 * self.n + w
-            return copy(dst, dst, t_s.at[sem, 0], t_r.at[sem, k], 2 * z + k // 8, c * 8 + lax.rem(k, 8))
+            return copy(dst, dst, t_s.at[sem, 0], t_r.at[sem, e * 8 + j], 2 * z + e, c * 8 + j)
 
         def sis(self, which, w):
             part = self.buf.at[which, :, :, self.rows(w)]
@@ -218,13 +232,15 @@
                 def _():
                     self.t_out(w, 0).wait_send()
 
-            def come(k):
-                @pl.when(jnp.logical_or(k // 8 != c, c * 8 + lax.rem(k, 8) != tp))
+            def come():
+                loop(NT, lambda k: self.t_in(w, k).wait_recv(), 1)
+
+                @pl.when(ht != c)
                 def _():
-                    self.t_in(w, k).wait_recv()
+                    self.t_in(w, 0).wait_recv()
 
             drains.append(drain)
-            comes["t%d" % w] = lambda: loop(NT, come)
+            comes["t%d" % w] = come
 
         def swap(self, w):
             self.sis(c, w).start()
@@ -258,11 +274,11 @@
         comes["last w%d" % a] = lambda: share(a, slot_sp, sister).wait_recv()
 
     def cot_out(d):
-        mo = lax.rem(m + d, MEM)
+        mo = plus(m, d, MEM)
         return copy(cpad.at[pl.ds(mo * TB, TB)], CT.at[m], g_s.at[3, mo, 0], g_r.at[3, m], MEM * p + mo, tp)
 
     def cot_in(d):
-        mo = lax.rem(m + d, MEM)
+        mo = plus(m, d, MEM)
         return copy(CT.at[mo], CT.at[mo], g_s.at[3, mo, 0], g_r.at[3, mo], MEM * p + mo, tp)
 
     loop(MEM, lambda d: cot_out(d).start(), 1)
@@ -326,22 +342,18 @@
     dec_swap(c).start()
     drains.append(lambda: dec_swap(c).wait_send())
     comes["dec"] = lambda: dec_swap(oc).wait_recv()
-    l_wg.wait()
-    l_wu.wait()
-    share_out(1)
-    share_out(2)
     share_on(0)
     if stop == 1:
         return finish()
 
     def ring(src, dst, n, own_src, send, d):
-        q = lax.rem(p + d, NP)
+        q = plus(p, d, NP)
         if send:
             return copy(src.at[q] if own_src else src, dst.at[p], z_s.at[n, q], z_r.at[n, p], MEM * q + m, tp)
         return copy(dst.at[q], dst.at[q], z_s.at[n, q], z_r.at[n, q], MEM * q + m, tp)
 
     def far(k):
-        return NP // 2 + (k + 1) // 2 * (1 - 2 * lax.rem(k, 2))
+        return NP // 2 + (k + 1) // 2 * (1 - 2 * (k % 2))
 
     def ring_start(src, dst, n, own_src, name):
         loop(NP - 1, lambda k: ring(src, dst, n, own_src, True, far(k)).start())
@@ -354,9 +366,13 @@
     bh = mm_nt(CT[0].reshape(RB, 128), WN[0])
     for g in range(1, MEM):
         bh = bh + mm_nt(CT[g].reshape(RB, 128), WN[g])
-    BS[...] = bh.reshape(NP, 8, FF)
+    BS[...] = folded(bh.reshape(NP, 8, FF)).astype(BF)
     BR[p] = BS[p]
     ring_start(BS, BR, 2, True, "bh sum")
+    l_wg.wait()
+    l_wu.wait()
+    share_out(1)
+    share_out(2)
     if stop == 2:
         return finish()
 
@@ -386,20 +402,24 @@
 
     def tsum_out(w, k):
         rows = pl.ds(w * half, half)
-        return copy(S2.at[lax.rem(k, 8), k // 8, rows], R2.at[tp, rows], t_s.at[4 + w, k], t_r.at[4 + w, tp],
-                    2 * z + k // 8, c * 8 + lax.rem(k, 8))
+        e = plus(c, k // 8, 2)
+        j = plus(jt, k % 8, 8)
+        return copy(S2.at[j, e, rows], R2.at[tp, rows], t_s.at[4 + w, k], t_r.at[4 + w, tp], 2 * z + e,
+                    c * 8 + j)
 
     def tsum_in(w, o):
         rows = pl.ds(w * half, half)
         return copy(R2.at[o, rows], R2.at[o, rows], t_s.at[4 + w, o], t_r.at[4 + w, o], 2 * z + ht, o)
 
-    def unless_me(k, fn):
-        @pl.when(jnp.logical_or(k // 8 != c, c * 8 + lax.rem(k, 8) != tp))
+    def tsum_drain(w):
+        loop(NT, lambda k: tsum_out(w, k).wait_send(), 1)
+
+        @pl.when(ht != c)
         def _():
-            fn()
+            tsum_out(w, 0).wait_send()
 
     def tsum_come(w):
-        loop(NT, lambda d: tsum_in(w, lax.rem(tp + d, NT)).wait_recv(), 1)
+        loop(NT, lambda d: tsum_in(w, plus(tp, d, NT)).wait_recv(), 1)
 
         @pl.when(ht != c)
         def _():
@@ -411,15 +431,18 @@
             both = mm(act[...], rhs).astype(BF)
             S2[:, 0, i] = both[:, :128].reshape(8, 16, 128)
             S2[:, 1, i] = both[:, 128:].reshape(8, 16, 128)
-        loop(NT, lambda k: unless_me(k, lambda: tsum_out(w, k).start()))
+        loop(NT, lambda k: tsum_out(w, k).start(), 1)
+
+        @pl.when(ht != c)
+        def _():
+            tsum_out(w, 0).start()
 
         @pl.when(ht == c)
         def _():
             rows = pl.ds(w * half, half)
             R2[tp, rows] = S2[jt, c, rows]
 
-        drains.append(functools.partial(
-            lambda w: loop(NT, lambda k: unless_me(k, lambda: tsum_out(w, k).wait_send())), w))
+        drains.append(functools.partial(tsum_drain, w))
         comes["ts%d" % w] = functools.partial(tsum_come, w)
     if stop == 4:
         return finish()
@@ -433,14 +456,13 @@
     drains.append(lambda: act_swap().wait_send())
     comes["act"] = lambda: to_sister(actf.at[oc], actf.at[oc], 7).wait_recv()
 
+    got("bh sum")
+    BG[p] = jnp.sum(BR[...].astype(F32), axis=0).astype(BF)
+    ring_start(BG.at[p], BG, 3, False, "bh")
     share_on(1)
     share_on(2)
     got("sis00")
     got("sis01")
-    got("bh sum")
-    BG[p] = jnp.sum(BR[...], axis=0)
-    ring_start(BG.at[p], BG, 3, False, "bh")
-
     def z_out(s):
         r = mirror(s)
         return copy(S3.at[s], R3.at[r], z_s.at[4, s], z_r.at[4, r], 2 * z_at(s) + c, tp)
@@ -468,34 +490,25 @@
     for a in (1, 2):
         got("sis w%d" % a)
         got("last w%d" % a)
-    for g in range(MEM):
-        WGT[g] = WG[g].T
-        WUT[g] = WU[g].T
+    for g in range(MEM // 2):
+        WGT[g] = WG[2 * g:2 * g + 2].reshape(256, FF).T
+        WUT[g] = WU[2 * g:2 * g + 2].reshape(256, FF).T
     got("z sum")
     bias = jnp.concatenate([bdec_ref[...], jnp.zeros((1, 128 - W), F32)], axis=1)
     rc16[...] = (jnp.sum(R3[...].astype(F32), axis=0) + bias).astype(BF)
     if stop == 6:
         return finish()
 
-    mt = tp // TB
-    slot = lax.rem(tp, TB)
-
     def rcopy(d):
-        o = lax.rem(tp + d, NT)
+        o = plus(tp, d, NT)
         return copy(rc16, RC.at[m, slot], t_s.at[6, o], t_r.at[6, m * TB + slot], MEM * p + mt, o)
 
-    def unless_self(k, fn):
-        g = k // TB
-        i = lax.rem(k, TB)
-
-        @pl.when(jnp.logical_or(g != m, m * TB + i != tp))
-        def _():
-            fn(k)
+    def member(k):
+        return plus(m, k // TB, MEM), plus(slot, k % TB, TB)
 
     def rwait(k):
-        g = k // TB
-        i = lax.rem(k, TB)
-        copy(rc16, RC.at[g, i], t_s.at[6, 0], t_r.at[6, k], MEM * p + g, m * TB + i).wait_recv()
+        g, i = member(k)
+        copy(rc16, RC.at[g, i], t_s.at[6, 0], t_r.at[6, g * TB + i], MEM * p + g, m * TB + i).wait_recv()
 
     loop(NT, lambda d: rcopy(d).start(), 1)
 
@@ -515,7 +528,12 @@
             rcopy(0).wait_send()
 
     drains.append(rdrain)
-    loop(MEM * TB, lambda k: unless_self(k, rwait))
+    loop(MEM * TB, rwait, 1)
+
+    @pl.when(mt != m)
+    def _():
+        rwait(0)
+
     if stop == 7:
         return finish()
 
@@ -548,57 +566,82 @@
     def cells(i):
         both_ = AG[i].astype(F32)
         gate_, up_ = both_[:8], both_[8:]
-        bh_ = BG[i]
+        bh_ = unfolded(BG[i].astype(F32))
         gelu_value, slope = gelu_parts(gate_)
         HID[i] = gelu_value * up_
         BGT[i] = bh_ * up_ * slope
         BUP[i] = bh_ * gelu_value
 
     loop(NP, cells)
-    hidden = HID[...].reshape(RB, FF).astype(BF)
     bgate = BGT[...].reshape(RB, FF).astype(BF)
     bup = BUP[...].reshape(RB, FF).astype(BF)
-    for g in range(MEM):
-        DS[g, :, 0] = mm(hidden, WN[g]).astype(BF).reshape(TB, 16, 128)
-        DS[g, :, 1] = (mm(bgate, WGT[g]) + mm(bup, WUT[g])).astype(BF).reshape(TB, 16, 128)
+    for g in range(MEM // 2):
+        both = (mm(bgate, WGT[g]) + mm(bup, WUT[g])).astype(BF)
+        DT[2 * g] = both[:, :128].reshape(TB, 16, 128)
+        DT[2 * g + 1] = both[:, 128:].reshape(TB, 16, 128)
     if stop == 10:
         return finish()
 
-    def dcopy(k):
-        g = k // TB
-        i = lax.rem(k, TB)
-        return copy(DS.at[g, i], DR.at[tp], t_s.at[7, k], t_r.at[7, tp], MEM * p + g, m * TB + i)
-
-    def dwait(d):
-        o = lax.rem(tp + d, NT)
-        copy(DR.at[o], DR.at[o], t_s.at[7, 0], t_r.at[7, o], MEM * p + mt, o).wait_recv()
-
-    loop(MEM * TB, lambda k: unless_self(k, lambda kk: dcopy(kk).start()))
-    drains.append(lambda: loop(MEM * TB, lambda k: unless_self(k, lambda kk: dcopy(kk).wait_send())))
-
-    @pl.when(mt == m)
-    def _():
-        DR[tp] = DS[m, slot]
-
-    @pl.when(mt != m)
-    def _():
-        dwait(0)
-
-    loop(NT, dwait, 1)
-    sums = jnp.sum(DR[...].astype(F32), axis=0)
-    recon = rc16[...].astype(F32)
-    back = cpad[tp].astype(F32) + sums[1] + recon - apad[tp].astype(F32)
-    ZB[0] = back.astype(BF)
+    class Sums:
+        def __init__(self, src, dst, n):
+            self.src, self.dst, self.n = src, dst, n
+
+        def out(self, k):
+            g, i = member(k)
+            return copy(self.src.at[g, i], self.dst.at[tp], t_s.at[self.n, k], t_r.at[self.n, tp], MEM * p + g,
+                        m * TB + i)
+
+        def come(self, d):
+            o = plus(tp, d, NT)
+            return copy(self.dst.at[o], self.dst.at[o], t_s.at[self.n, 0], t_r.at[self.n, o], MEM * p + mt, o)
+
+        def start(self, name):
+            loop(MEM * TB, lambda k: self.out(k).start(), 1)
+
+            @pl.when(mt != m)
+            def _():
+                self.out(0).start()
+
+            @pl.when(mt == m)
+            def _():
+                self.dst[tp] = self.src[m, slot]
+
+            def drain():
+                loop(MEM * TB, lambda k: self.out(k).wait_send(), 1)
+
+                @pl.when(mt != m)
+                def _():
+                    self.out(0).wait_send()
+
+            def wait():
+                loop(NT, lambda d: self.come(d).wait_recv(), 1)
+
+                @pl.when(mt != m)
+                def _():
+                    self.come(0).wait_recv()
+
+            drains.append(drain)
+            comes[name] = wait
+
+    Sums(DT, RT, 7).start("through")
+    hidden = HID[...].reshape(RB, FF).astype(BF)
+    for g in range(MEM // 2):
+        both = mm(hidden, jnp.concatenate([WN[2 * g], WN[2 * g + 1]], axis=1)).astype(BF)
+        DS[2 * g] = both[:, :128].reshape(TB, 16, 128)
+        DS[2 * g + 1] = both[:, 128:].reshape(TB, 16, 128)
+    base = cpad[tp].astype(F32) + rc16[...].astype(F32) - apad[tp].astype(F32)
+    got("through")
+    ZB[0] = (base + jnp.sum(RT[...].astype(F32), axis=0)).astype(BF)
     if stop == 11:
         return finish()
 
     gy = Gather(ZB, Y, 1)
     gy.start()
-    out_ref[...] = (recon + sums[0]).astype(BF)[:, :W]
     gy.forward(0)
     if stop == 12:
         return finish()
     gy.forward(1)
+    Sums(DS, DR, 8).start("down")
     if stop == 13:
         return finish()
 
@@ -610,6 +653,13 @@
             lhs = jnp.concatenate([Y[h, :, 0, i].reshape(128, 128), Y[h, :, 1, i].reshape(128, 128)], axis=1)
             s = s + mm(lhs, WDT[i].reshape(256, 128))
         acc[h] = s
+
+    def dec_part(lo, hi):
+        for i in range(lo, hi):
+            rhs = jnp.concatenate([Y[:, :, h, i].reshape(256, 128) for h in range(2)], axis=1)
+            both = mm(actt[...], rhs).astype(BF)
+            gdec_ref[2 * z_at(i)] = both[:, :128]
+            gdec_ref[2 * z_at(i) + 1] = both[:, 128:]
 
     got("t0")
     gy.swap(0)
@@ -619,6 +669,9 @@
     back_part(c, NEAR, NZ)
     got("sis10")
     back_part(oc, 0, NEAR)
+    dec_part(0, NEAR)
+    got("down")
+    out_ref[...] = (rc16[...].astype(F32) + jnp.sum(DR[...].astype(F32), axis=0)).astype(BF)[:, :W]
     got("sis11")
     back_part(oc, NEAR, NZ)
     if stop == 14:
@@ -630,15 +683,22 @@
 
     def enc_grad(k):
         h = k // NZ
-        s = lax.rem(k, NZ)
+        s = k % NZ
         rows = pl.ds(pl.multiple_of((2 * z_at(s) + h) * W, 16), W)
         genc_ref[rows, :] = mm(XT[h, s], actf[...].reshape(256, 128))[:W].astype(BF)
 
-    lax.fori_loop(0, 2 * NZ, lambda k, n: (enc_grad(k), n)[1], 0, unroll=4)
+    loop(2 * NZ, enc_grad)
+    dec_part(NEAR, NZ)
+    finish()
+
+
+def hand_on(out_in, genc_in, gencb_in, gdec_in, gdecb_in, out_ref, genc_ref, gencb_ref, gdec_ref, gdecb_ref):
+    out_ref[...] = out_in[...]
+    genc_ref[...] = genc_in[...]
+    gencb_ref[...] = gencb_in[...]
+    gdecb_ref[...] = gdecb_in[...]
     for i in range(2 * NZ):
-        y = Y[:, :, i % 2, slot_of(i // 2 - z)].reshape(256, 128)
-        gdec_ref[:, i * W:(i + 1) * W] = mm(actt[...], y)[:, :W].astype(BF)
-    finish()
+        gdec_ref[:, i * W:(i + 1) * W] = gdec_in[i][:, :W]
 
 
 def step(activations, indices, w_enc, b_enc, w_dec, b_dec, w_gate, w_up, w_down, cotangent, stop=99, cid=1):
@@ -646,15 +706,17 @@
     dma = pltpu.SemaphoreType.DMA
     inside = pl.BlockSpec(memory_space=pltpu.VMEM)
     outside = pl.BlockSpec(memory_space=pl.ANY)
-    return pl.pallas_call(
+    shapes = (
+        jax.ShapeDtypeStruct((16, W), BF),
+        jax.ShapeDtypeStruct((2 * NZ * W, 128), BF),
+        jax.ShapeDtypeStruct((128,), F32),
+        jax.ShapeDtypeStruct((128, 2 * NZ * W), BF),
+        jax.ShapeDtypeStruct((W,), F32),
+    )
+    held = shapes[:3] + (jax.ShapeDtypeStruct((2 * NZ, 128, 128), BF),) + shapes[4:]
+    results = pl.pallas_call(
         functools.partial(kernel, stop),
-        out_shape=(
-            jax.ShapeDtypeStruct((16, W), BF),
-            jax.ShapeDtypeStruct((2 * NZ * W, 128), BF),
-            jax.ShapeDtypeStruct((128,), F32),
-            jax.ShapeDtypeStruct((128, 2 * NZ * W), BF),
-            jax.ShapeDtypeStruct((W,), F32),
-        ),
+        out_shape=held,
         in_specs=[inside, inside, outside, inside, outside, inside, outside, outside, outside, inside],
         out_specs=[inside] * 5,
         scratch_shapes=[
@@ -683,18 +745,20 @@
             vm((MEM, TB, 16, 128), BF),
             vm((MEM, 128, FF), BF),
             vm((MEM, 128, FF), BF),
-            vm((MEM, FF, 128), BF),
-            vm((MEM, FF, 128), BF),
+            vm((MEM // 2, FF, 256), BF),
+            vm((MEM // 2, FF, 256), BF),
             vm((MEM, FF, 128), BF),
             vm((MEM, TB, 16, 128), BF),
-            vm((NP, 8, FF), F32),
-            vm((NP, 8, FF), F32),
-            vm((NP, 8, FF), F32),
+            vm((NP, 16, 512), BF),
+            vm((NP, 16, 512), BF),
+            vm((NP, 16, 512), BF),
             vm((NP, 16, FF), BF),
             vm((NP, 16, FF), BF),
             vm((NP, 16, FF), BF),
-            vm((MEM, TB, 2, 16, 128), BF),
-            vm((NT, 2, 16, 128), BF),
+            vm((MEM, TB, 16, 128), BF),
+            vm((NT, 16, 128), BF),
+            vm((MEM, TB, 16, 128), BF),
+            vm((NT, 16, 128), BF),
             vm((NP, 8, FF), F32),
             vm((NP, 8, FF), F32),
             vm((NP, 8, FF), F32),
@@ -702,7 +766,7 @@
             vm((128, FF), BF),
             dma((9,)), dma((9,)),
             dma((7, NZ)), dma((7, NZ)),
-            dma((8, NT)), dma((8, NT)),
+            dma((9, NT)), dma((9, NT)),
             dma((4, MEM, 2)), dma((4, MEM)),
             dma((4 + 2 * NZ,)),
         ],
@@ -715,6 +779,14 @@
         activations.T, indices.T, w_enc, b_enc.reshape(1, 128), w_dec, b_dec.reshape(1, W),
         w_gate, w_up, w_down.T, cotangent.T,
     )
+    return pl.pallas_call(
+        hand_on,
+        out_shape=shapes,
+        in_specs=[inside] * 5,
+        out_specs=[inside] * 5,
+        compiler_params=pltpu.CompilerParams(vmem_limit_bytes=60 * 2**20),
+        name="results",
+    )(*results)
 
 
 def solution(mesh):

time: 140 us -> 125 us (0.89)
  Pallas kernels: 133 us -> 125 us
  local copies, waits for them, and re-layouts: 5.46 us -> 0 us
    pallas_call x1 -> x2, Pallas kernels: 133 us -> 125 us  [the longest x1 121 us: step(): pl.pallas_call(functools.partial(kernel, stop), out_shape=held, in_specs=...]
    unnamed x13 -> x0, local copies, waits for them, and re-layouts: 5.46 us -> none
where the time goes in v3:
time: 125 us
  Pallas kernels  125 us (100%)
    pallas_call x1, Pallas kernels, step(): pl.pallas_call(functools.partial(kernel, stop), out_shape=held, in_specs=...  121 us
    pallas_call x1, Pallas kernels, step(): pl.pallas_call(hand_on, out_shape=shapes, in_specs=[inside] * 5, out_spec...  3.27 us

profile of v3, /device:TPU:1, one launch (start us, length us, event | category | flops | bytes accessed | tf_op | source)
XLA Modules:
  0.0 125.2 jit_solution(8039836690430144962)
XLA Ops:
  0.6 121.3 %sae_step.1 = (bf16[16,112]{1,0:T(8,128)(2,1)}, bf16[3584,128]{1,0:T(8,128)(2,1)}, f32[128]{0:T(128)}, bf16[32,128,128]{2,1,0:T(8,128)(2,1)}, f32[112]{0:T(128)}) custom-call(bf16[112,256]{1,0:T(8,128)(2,1)} %bitcast.8, s32[64,256]{1,0:T(8,128)} %bitcast.7, bf16[3584,128]{1,0:T(8,128)(2,1)} %wenc_ref.1, f32[1,128]{1,0:T(1,128)} %bitcast.10, ...), custom_call_target="tpu_custom_call" | custom-call | flops 2000000000 | bytes 6000000 | tf_op jit(solution)/shard_map/sae_step/pallas_call | solution.py:717
  122.0 3.3 %results.1 = (bf16[16,112]{1,0:T(8,128)(2,1)}, bf16[3584,128]{1,0:T(8,128)(2,1)}, f32[128]{0:T(128)}, bf16[128,3584]{1,0:T(8,128)(2,1)}, f32[112]{0:T(128)}) custom-call(bf16[16,112]{1,0:T(8,128)(2,1)} %get-tuple-element.10.out_in, bf16[3584,128]{1,0:T(8,128)(2,1)} %get-tuple-element.11.genc_in, f32[128]{0:T(128)} %get-tuple-element.12.gencb_in, ...), custom_call_target="tpu_custom_call" | custom-call | tf_op jit(solution)/shard_map/results/pallas_call | solution.py:782

commit v4 on v3

--- a/solution.py
+++ b/solution.py
@@ -17,7 +17,8 @@
 RB = 16 * TB
 W = 112
 FF = 896
-NEAR = 9
+PARTS = ((0, 8), (8, 8))
+PAD = 128 - W
 BF = jnp.bfloat16
 F32 = jnp.float32
 
@@ -59,6 +60,15 @@
     return jnp.maximum(jnp.where(d <= NZ // 2, 2 * d - 1, 2 * (NZ - d)), 0)
 
 
+def carry(block, last, k):
+    return jnp.concatenate([block[:, :W], last[:, k * PAD:(k + 1) * PAD]], axis=1)
+
+
+def carried(blocks):
+    rest = jnp.zeros((blocks[0].shape[0], PAD), blocks[0].dtype)
+    return jnp.concatenate([b[:, W:] for b in blocks] + [rest], axis=1)
+
+
 def folded(v):
     rest = jnp.concatenate([v[..., 512:], jnp.zeros(v.shape[:-1] + (128,), v.dtype)], axis=-1)
     return jnp.concatenate([v[..., :512], rest], axis=-2)
@@ -74,12 +84,12 @@
 
 
 def kernel(
-    stop,
-    at_ref, idxt_ref, wenc_ref, benc_ref, wdec_ref, bdec_ref, wg_ref, wu_ref, wnt_ref, cott_ref,
-    out_ref, genc_ref, gencb_ref, gdec_ref, gdecb_ref,
-    apad, cpad, ZA, ZB, X, Y, XT, WE, WD, WDT, hit, hit2, bias2, act, actf, actt, acc, S2, R2, S3, R3, rc16, RC,
+    at_in, idxt_in, wenc_ref, benc_in, wdec_ref, bdec_in, wg_ref, wu_ref, wnt_ref, cott_in,
+    out_ref, genc_out, gencb_ref, gdec_out, gdecb_ref,
+    at_ref, idxt_ref, benc_ref, bdec_ref, cott_ref, genc_ref, gdec_ref,
+    apad, cpad, ZA, ZB, ZAP, ZBP, X, Y, XT, WE, WD, WDT, hit, hit2, bias2, act, actf, actt, acc, S2, R2, S3, R3, rc16, RC,
     WG, WU, WGT, WUT, WN, CT, BS, BR, BG, CS, CR, AG, DS, DR, DT, RT, HID, BGT, BUP, wdec, wnt,
-    s_s, s_r, z_s, z_r, t_s, t_r, g_s, g_r, l_s,
+    s_s, s_r, z_s, z_r, t_s, t_r, g_s, g_r, l_s, o_s,
 ):
     lat = lax.axis_index("lat")
     tp = lax.axis_index("tp")
@@ -143,11 +153,17 @@
         rows = pl.ds(pl.multiple_of((2 * z_at(s) + h) * W, 16), W)
         return pltpu.make_async_copy(wenc_ref.at[rows], WE.at[c, s, h, top], l_s.at[4 + k])
 
+    def l_small(k):
+        pairs = ((at_in, at_ref), (cott_in, cott_ref), (idxt_in, idxt_ref), (benc_in, benc_ref), (bdec_in, bdec_ref))
+        return pltpu.make_async_copy(pairs[k][0], pairs[k][1], o_s.at[k])
+
+    loop(5, lambda k: l_small(k).start())
     l_wnt.start()
-    loop(2 * NZ, lambda k: l_we(k).start())
-    l_wd.start()
     l_wg.start()
     l_wu.start()
+    l_wd.start()
+    loop(2 * NZ, lambda k: l_we(k).start())
+    loop(5, lambda k: l_small(k).wait())
 
     fill = jnp.zeros((128 - W, 256), BF)
     apad[...] = jnp.concatenate([at_ref[...], fill], axis=0).T.reshape(NT, 16, 128)
@@ -168,17 +184,21 @@
     l_wnt.wait()
     WN[m] = wnt[...].T
 
+    ids_col = (lat * NT + tp) * 128 + lax.broadcasted_iota(jnp.int32, (128, 256), 0)
+
+    def one_hit(j, found):
+        return jnp.where(idxt_ref[pl.ds(j, 1), :] == ids_col, 1.0, found)
+
+    hit[...] = lax.fori_loop(0, idxt_ref.shape[0], one_hit, jnp.zeros((128, 256), F32), unroll=8).T
+    other_rows = pl.ds(pl.multiple_of(oc * 128, 128), 128)
+    own_rows = pl.ds(pl.multiple_of(c * 128, 128), 128)
+    hit2[c] = hit[own_rows, :]
+
     pl.semaphore_wait(bar, NZ - 1 + MEM * NT - 1)
-    if stop == 0:
-        loop(2 * NZ, lambda k: l_we(k).wait())
-        l_wg.wait()
-        l_wu.wait()
-        l_wd.wait()
-        return finish()
 
     class Gather:
-        def __init__(self, zb, buf, n):
-            self.zb, self.buf, self.n = zb, buf, n
+        def __init__(self, zb, zp, buf, n):
+            self.zb, self.zp, self.buf, self.n = zb, zp, buf, n
 
         def z_out(self, s):
             r = mirror(s)
@@ -188,33 +208,37 @@
             return copy(self.zb.at[s], self.zb.at[s], z_s.at[self.n, s], z_r.at[self.n, s], 2 * z_at(s) + c, tp)
 
         def rows(self, w):
-            return pl.ds(0, NEAR) if w == 0 else pl.ds(NEAR, NZ - NEAR)
+            return pl.ds(8 * w, 7)
 
         def t_out(self, w, d):
             to = plus(tp, d, NT)
-            sem = 2 * self.n + w
-            return copy(self.zb.at[self.rows(w)], self.buf.at[ht, jt, c, self.rows(w)],
+            sem = 3 * self.n + w
+            return copy(self.zp.at[self.rows(w)], self.buf.at[ht, jt, c, self.rows(w)],
                         t_s.at[sem, to], t_r.at[sem, c * 8 + jt], 2 * z + ht, to)
 
         def t_in(self, w, k):
             e = plus(c, k // 8, 2)
             j = plus(jt, k % 8, 8)
             dst = self.buf.at[c, j, e, self.rows(w)]
-            sem = 2 * self.n + w
+            sem = 3 * self.n + w
             return copy(dst, dst, t_s.at[sem, 0], t_r.at[sem, e * 8 + j], 2 * z + e, c * 8 + j)
 
         def sis(self, which, w):
             part = self.buf.at[which, :, :, self.rows(w)]
-            return to_sister(part, part, 2 * self.n + w)
+            return to_sister(part, part, 3 * self.n + w)
 
         def start(self):
             loop(NZ - 1, lambda k: self.z_out(NZ - 1 - k).start())
             drains.append(lambda: loop(NZ, lambda s: self.z_out(s).wait_send(), 1))
-            comes["z0"] = lambda: loop(NEAR, lambda s: self.z_in(s).wait_recv(), 1)
-            comes["z1"] = lambda: loop(NZ, lambda s: self.z_in(s).wait_recv(), NEAR)
+            for w, (lo, n) in enumerate(PARTS):
+                comes["z%d" % w] = functools.partial(
+                    loop, lo + n, lambda s: self.z_in(s).wait_recv(), max(lo, 1))
 
         def forward(self, w):
             got("z%d" % w)
+            last = self.zb[8 * w + 7]
+            for k in range(7):
+                self.zp[8 * w + k] = carry(self.zb[8 * w + k], last, k)
             loop(NT, lambda d: self.t_out(w, d).start(), 1)
 
             @pl.when(ht != c)
@@ -223,7 +247,7 @@
 
             @pl.when(ht == c)
             def _():
-                self.buf[c, jt, c, self.rows(w)] = self.zb[self.rows(w)]
+                self.buf[c, jt, c, self.rows(w)] = self.zp[self.rows(w)]
 
             def drain():
                 loop(NT, lambda d: self.t_out(w, d).wait_send(), 1)
@@ -241,13 +265,18 @@
 
             drains.append(drain)
             comes["t%d" % w] = come
+
+        def unpack(self, h, w):
+            for e in range(2):
+                blocks = [self.buf[h, :, e, 8 * w + k].reshape(128, 128) for k in range(7)]
+                self.buf[h, :, e, 8 * w + 7] = carried(blocks).reshape(8, 16, 128)
 
         def swap(self, w):
             self.sis(c, w).start()
             drains.append(lambda: self.sis(c, w).wait_send())
             comes["sis%d%d" % (self.n, w)] = lambda: self.sis(oc, w).wait_recv()
 
-    ga = Gather(ZA, X, 0)
+    ga = Gather(ZA, ZAP, X, 0)
     ga.start()
 
     def weight(a, i):
@@ -286,35 +315,25 @@
     comes["cot"] = lambda: loop(MEM, lambda d: cot_in(d).wait_recv(), 1)
     share_out(0)
 
-    ids_col = (lat * NT + tp) * 128 + lax.broadcasted_iota(jnp.int32, (128, 256), 0)
-
-    def one_hit(j, found):
-        return jnp.where(idxt_ref[pl.ds(j, 1), :] == ids_col, 1.0, found)
-
-    hit[...] = lax.fori_loop(0, idxt_ref.shape[0], one_hit, jnp.zeros((128, 256), F32), unroll=8).T
-    other_rows = pl.ds(pl.multiple_of(oc * 128, 128), 128)
-    own_rows = pl.ds(pl.multiple_of(c * 128, 128), 128)
-    hit2[c] = hit[own_rows, :]
-
     def hit_swap():
-        return to_sister(hit.at[other_rows], hit2.at[c], 4)
+        return to_sister(hit.at[other_rows], hit2.at[c], 6)
 
     hit_swap().start()
     drains.append(lambda: hit_swap().wait_send())
     bias2[c] = jnp.broadcast_to(benc_ref[...], (8, 128))
 
     def bias_swap(i):
-        return to_sister(bias2.at[i], bias2.at[i], 8)
+        return to_sister(bias2.at[i], bias2.at[i], 10)
 
     bias_swap(c).start()
     drains.append(lambda: bias_swap(c).wait_send())
     comes["bias"] = lambda: bias_swap(oc).wait_recv()
-    comes["hit"] = lambda: to_sister(hit2.at[oc], hit2.at[oc], 4).wait_recv()
+    comes["hit"] = lambda: to_sister(hit2.at[oc], hit2.at[oc], 6).wait_recv()
 
     loop(2 * NZ, lambda k: l_we(k).wait())
 
     def enc_swap(i):
-        return to_sister(WE.at[i], WE.at[i], 5)
+        return to_sister(WE.at[i], WE.at[i], 7)
 
     enc_swap(c).start()
     drains.append(lambda: enc_swap(c).wait_send())
@@ -337,14 +356,12 @@
         dec_block(i)
 
     def dec_swap(i):
-        return to_sister(WD.at[i], WD.at[i], 6)
+        return to_sister(WD.at[i], WD.at[i], 8)
 
     dec_swap(c).start()
     drains.append(lambda: dec_swap(c).wait_send())
     comes["dec"] = lambda: dec_swap(oc).wait_recv()
     share_on(0)
-    if stop == 1:
-        return finish()
 
     def ring(src, dst, n, own_src, send, d):
         q = plus(p, d, NP)
@@ -373,8 +390,6 @@
     l_wu.wait()
     share_out(1)
     share_out(2)
-    if stop == 2:
-        return finish()
 
     def pre_part(start, lo, hi):
         pre = start
@@ -387,29 +402,26 @@
     got("bias")
     got("enc")
     got("hit")
-    got("t0")
-    ga.swap(0)
-    pre = pre_part(jnp.concatenate([bias2[0, 0:1], bias2[1, 0:1]], axis=1), 0, NEAR)
-    got("t1")
-    ga.swap(1)
-    pre = pre_part(pre, NEAR, NZ)
+    pre = jnp.concatenate([bias2[0, 0:1], bias2[1, 0:1]], axis=1)
+    for w, (lo, n) in enumerate(PARTS):
+        got("t%d" % w)
+        ga.swap(w)
+        ga.unpack(c, w)
+        pre = pre_part(pre, lo, lo + n)
     act[...] = (pre * jnp.concatenate([hit2[0], hit2[1]], axis=1)).astype(BF)
-    if stop == 3:
-        return finish()
 
     got("dec")
-    half = NZ // 2
 
     def tsum_out(w, k):
-        rows = pl.ds(w * half, half)
+        rows = pl.ds(8 * w, 7)
         e = plus(c, k // 8, 2)
         j = plus(jt, k % 8, 8)
-        return copy(S2.at[j, e, rows], R2.at[tp, rows], t_s.at[4 + w, k], t_r.at[4 + w, tp], 2 * z + e,
+        return copy(S2.at[j, e, rows], R2.at[tp, rows], t_s.at[6 + w, k], t_r.at[6 + w, tp], 2 * z + e,
                     c * 8 + j)
 
     def tsum_in(w, o):
-        rows = pl.ds(w * half, half)
-        return copy(R2.at[o, rows], R2.at[o, rows], t_s.at[4 + w, o], t_r.at[4 + w, o], 2 * z + ht, o)
+        rows = pl.ds(8 * w, 7)
+        return copy(R2.at[o, rows], R2.at[o, rows], t_s.at[6 + w, o], t_r.at[6 + w, o], 2 * z + ht, o)
 
     def tsum_drain(w):
         loop(NT, lambda k: tsum_out(w, k).wait_send(), 1)
@@ -425,12 +437,17 @@
         def _():
             tsum_in(w, tp).wait_recv()
 
+    def partial(i):
+        rhs = jnp.concatenate([jnp.concatenate([WD[0, e, i], WD[1, e, i]], axis=0) for e in (0, 1)], axis=1)
+        both = mm(act[...], rhs)
+        return both[:, :128], both[:, 128:]
+
     for w in (1, 0):
-        for i in range(w * half, (w + 1) * half):
-            rhs = jnp.concatenate([jnp.concatenate([WD[0, e, i], WD[1, e, i]], axis=0) for e in (0, 1)], axis=1)
-            both = mm(act[...], rhs).astype(BF)
-            S2[:, 0, i] = both[:, :128].reshape(8, 16, 128)
-            S2[:, 1, i] = both[:, 128:].reshape(8, 16, 128)
+        last = partial(8 * w + 7)
+        for k in range(7):
+            here = partial(8 * w + k)
+            for e in range(2):
+                S2[:, e, 8 * w + k] = carry(here[e], last[e], k).astype(BF).reshape(8, 16, 128)
         loop(NT, lambda k: tsum_out(w, k).start(), 1)
 
         @pl.when(ht != c)
@@ -439,30 +456,29 @@
 
         @pl.when(ht == c)
         def _():
-            rows = pl.ds(w * half, half)
+            rows = pl.ds(8 * w, 7)
             R2[tp, rows] = S2[jt, c, rows]
 
         drains.append(functools.partial(tsum_drain, w))
         comes["ts%d" % w] = functools.partial(tsum_come, w)
-    if stop == 4:
-        return finish()
 
     actf[c] = act[:, pl.ds(pl.multiple_of(c * 128, 128), 128)]
 
     def act_swap():
-        return to_sister(act.at[:, pl.ds(pl.multiple_of(oc * 128, 128), 128)], actf.at[c], 7)
+        return to_sister(act.at[:, pl.ds(pl.multiple_of(oc * 128, 128), 128)], actf.at[c], 9)
 
     act_swap().start()
     drains.append(lambda: act_swap().wait_send())
-    comes["act"] = lambda: to_sister(actf.at[oc], actf.at[oc], 7).wait_recv()
+    comes["act"] = lambda: to_sister(actf.at[oc], actf.at[oc], 9).wait_recv()
 
     got("bh sum")
     BG[p] = jnp.sum(BR[...].astype(F32), axis=0).astype(BF)
     ring_start(BG.at[p], BG, 3, False, "bh")
     share_on(1)
     share_on(2)
-    got("sis00")
-    got("sis01")
+    for w in range(2):
+        got("sis0%d" % w)
+        ga.unpack(oc, w)
     def z_out(s):
         r = mirror(s)
         return copy(S3.at[s], R3.at[r], z_s.at[4, s], z_r.at[4, r], 2 * z_at(s) + c, tp)
@@ -470,23 +486,17 @@
     def z_in(s):
         return copy(R3.at[s], R3.at[s], z_s.at[4, s], z_r.at[4, s], 2 * z_at(s) + c, tp)
 
-    def tadd(s):
-        S3[s] = jnp.sum(R2[:, s].astype(F32), axis=0).astype(BF)
-
-    def far_sum(k):
-        tadd(NZ - 1 - k)
-        z_out(NZ - 1 - k).start()
-
-    got("ts1")
-    loop(half, far_sum)
-    got("ts0")
-    loop(half - 1, lambda k: far_sum(k + half))
-    tadd(0)
+    for w in (1, 0):
+        got("ts%d" % w)
+        terms = [jnp.sum(R2[:, 8 * w + k].astype(F32), axis=0) for k in range(7)]
+        terms.append(carried(terms))
+        for k in reversed(range(8)):
+            S3[8 * w + k] = terms[k].astype(BF)
+            if 8 * w + k:
+                z_out(8 * w + k).start()
     R3[0] = S3[0]
     drains.append(lambda: loop(NZ, lambda s: z_out(s).wait_send(), 1))
     comes["z sum"] = lambda: loop(NZ, lambda s: z_in(s).wait_recv(), 1)
-    if stop == 5:
-        return finish()
     for a in (1, 2):
         got("sis w%d" % a)
         got("last w%d" % a)
@@ -496,19 +506,17 @@
     got("z sum")
     bias = jnp.concatenate([bdec_ref[...], jnp.zeros((1, 128 - W), F32)], axis=1)
     rc16[...] = (jnp.sum(R3[...].astype(F32), axis=0) + bias).astype(BF)
-    if stop == 6:
-        return finish()
 
     def rcopy(d):
         o = plus(tp, d, NT)
-        return copy(rc16, RC.at[m, slot], t_s.at[6, o], t_r.at[6, m * TB + slot], MEM * p + mt, o)
+        return copy(rc16, RC.at[m, slot], t_s.at[9, o], t_r.at[9, m * TB + slot], MEM * p + mt, o)
 
     def member(k):
         return plus(m, k // TB, MEM), plus(slot, k % TB, TB)
 
     def rwait(k):
         g, i = member(k)
-        copy(rc16, RC.at[g, i], t_s.at[6, 0], t_r.at[6, g * TB + i], MEM * p + g, m * TB + i).wait_recv()
+        copy(rc16, RC.at[g, i], t_s.at[9, 0], t_r.at[9, g * TB + i], MEM * p + g, m * TB + i).wait_recv()
 
     loop(NT, lambda d: rcopy(d).start(), 1)
 
@@ -534,8 +542,6 @@
     def _():
         rwait(0)
 
-    if stop == 7:
-        return finish()
 
     def pairs(i):
         return jnp.concatenate([RC[2 * i].reshape(RB, 128), RC[2 * i + 1].reshape(RB, 128)], axis=1)
@@ -553,15 +559,11 @@
             XT[h, i] = X[:, :, h, i].reshape(256, 128).T
     got("act")
     actt[...] = actf[...].reshape(256, 128).T
-    if stop == 8:
-        return finish()
     got("gate sum")
     AG[p] = jnp.sum(CR[...].astype(F32), axis=0).astype(BF)
     ring_start(AG.at[p], AG, 6, False, "gate")
     got("bh")
     got("gate")
-    if stop == 9:
-        return finish()
 
     def cells(i):
         both_ = AG[i].astype(F32)
@@ -579,8 +581,6 @@
         both = (mm(bgate, WGT[g]) + mm(bup, WUT[g])).astype(BF)
         DT[2 * g] = both[:, :128].reshape(TB, 16, 128)
         DT[2 * g + 1] = both[:, 128:].reshape(TB, 16, 128)
-    if stop == 10:
-        return finish()
 
     class Sums:
         def __init__(self, src, dst, n):
@@ -623,7 +623,7 @@
             drains.append(drain)
             comes[name] = wait
 
-    Sums(DT, RT, 7).start("through")
+    Sums(DT, RT, 10).start("through")
     hidden = HID[...].reshape(RB, FF).astype(BF)
     for g in range(MEM // 2):
         both = mm(hidden, jnp.concatenate([WN[2 * g], WN[2 * g + 1]], axis=1)).astype(BF)
@@ -632,76 +632,84 @@
     base = cpad[tp].astype(F32) + rc16[...].astype(F32) - apad[tp].astype(F32)
     got("through")
     ZB[0] = (base + jnp.sum(RT[...].astype(F32), axis=0)).astype(BF)
-    if stop == 11:
-        return finish()
-
-    gy = Gather(ZB, Y, 1)
+
+    gy = Gather(ZB, ZBP, Y, 1)
     gy.start()
     gy.forward(0)
-    if stop == 12:
-        return finish()
     gy.forward(1)
-    Sums(DS, DR, 8).start("down")
-    if stop == 13:
-        return finish()
+    Sums(DS, DR, 11).start("down")
 
     acc[...] = jnp.zeros_like(acc)
 
-    def back_part(h, lo, hi):
+    def back_part(h, w):
         s = acc[h]
-        for i in range(lo, hi):
+        for i in range(PARTS[w][0], sum(PARTS[w])):
             lhs = jnp.concatenate([Y[h, :, 0, i].reshape(128, 128), Y[h, :, 1, i].reshape(128, 128)], axis=1)
             s = s + mm(lhs, WDT[i].reshape(256, 128))
         acc[h] = s
 
-    def dec_part(lo, hi):
-        for i in range(lo, hi):
+    def leave(src, dst, n):
+        cp = pltpu.make_async_copy(src, dst, o_s.at[n])
+        cp.start()
+        drains.append(cp.wait)
+
+    def dec_part(w):
+        for i in range(PARTS[w][0], sum(PARTS[w])):
             rhs = jnp.concatenate([Y[:, :, h, i].reshape(256, 128) for h in range(2)], axis=1)
             both = mm(actt[...], rhs).astype(BF)
-            gdec_ref[2 * z_at(i)] = both[:, :128]
-            gdec_ref[2 * z_at(i) + 1] = both[:, 128:]
-
-    got("t0")
-    gy.swap(0)
-    back_part(c, 0, NEAR)
-    got("t1")
-    gy.swap(1)
-    back_part(c, NEAR, NZ)
+            gdec_ref[i, 0] = both[:, :128]
+            gdec_ref[i, 1] = both[:, 128:]
+        part = pl.ds(*PARTS[w])
+        leave(gdec_ref.at[part], gdec_out.at[part], 5 + w)
+
+    def arrived(w):
+        got("t%d" % w)
+        gy.swap(w)
+        gy.unpack(c, w)
+        back_part(c, w)
+
+    arrived(0)
     got("sis10")
-    back_part(oc, 0, NEAR)
-    dec_part(0, NEAR)
+    gy.unpack(oc, 0)
+    back_part(oc, 0)
+    dec_part(0)
     got("down")
     out_ref[...] = (rc16[...].astype(F32) + jnp.sum(DR[...].astype(F32), axis=0)).astype(BF)[:, :W]
+    arrived(1)
     got("sis11")
-    back_part(oc, NEAR, NZ)
-    if stop == 14:
-        return finish()
+    gy.unpack(oc, 1)
+    back_part(oc, 1)
     bact = (acc[...].reshape(256, 128) * hit[...]).astype(BF)
     gencb_ref[...] = jnp.sum(bact.astype(F32), axis=0)
     gdecb_ref[...] = jnp.sum(Y[:, :, c, 0].reshape(256, 128).astype(F32), axis=0)[:W]
     actf[...] = bact.reshape(2, 128, 128)
 
     def enc_grad(k):
-        h = k // NZ
-        s = k % NZ
-        rows = pl.ds(pl.multiple_of((2 * z_at(s) + h) * W, 16), W)
-        genc_ref[rows, :] = mm(XT[h, s], actf[...].reshape(256, 128))[:W].astype(BF)
-
-    loop(2 * NZ, enc_grad)
-    dec_part(NEAR, NZ)
+        h = k // 4
+        first = k % 4 * 4
+        four = mm(XT[h, first:first + 4].reshape(512, 256), actf[...].reshape(256, 128)).astype(BF)
+        for i in range(4):
+            genc_ref[h, first + i] = four[128 * i:128 * i + W]
+        part = pl.ds(first, 4)
+        leave(genc_ref.at[h, part], genc_out.at[h, part], 7 + k)
+
+    loop(8, enc_grad)
+    dec_part(1)
     finish()
 
 
 def hand_on(out_in, genc_in, gencb_in, gdec_in, gdecb_in, out_ref, genc_ref, gencb_ref, gdec_ref, gdecb_ref):
+    z = lax.axis_index("lat") // 2
     out_ref[...] = out_in[...]
-    genc_ref[...] = genc_in[...]
     gencb_ref[...] = gencb_in[...]
     gdecb_ref[...] = gdecb_in[...]
     for i in range(2 * NZ):
-        gdec_ref[:, i * W:(i + 1) * W] = gdec_in[i][:, :W]
-
-
-def step(activations, indices, w_enc, b_enc, w_dec, b_dec, w_gate, w_up, w_down, cotangent, stop=99, cid=1):
+        s = slot_of(i // 2 - z)
+        genc_ref[i * W:(i + 1) * W, :] = genc_in[i % 2, s]
+        gdec_ref[:, i * W:(i + 1) * W] = gdec_in[s, i % 2][:, :W]
+
+
+def step(activations, indices, w_enc, b_enc, w_dec, b_dec, w_gate, w_up, w_down, cotangent):
     vm = pltpu.VMEM
     dma = pltpu.SemaphoreType.DMA
     inside = pl.BlockSpec(memory_space=pltpu.VMEM)
@@ -713,15 +721,26 @@
         jax.ShapeDtypeStruct((128, 2 * NZ * W), BF),
         jax.ShapeDtypeStruct((W,), F32),
     )
-    held = shapes[:3] + (jax.ShapeDtypeStruct((2 * NZ, 128, 128), BF),) + shapes[4:]
+    genc_held = jax.ShapeDtypeStruct((2, NZ, W, 128), BF)
+    gdec_held = jax.ShapeDtypeStruct((NZ, 2, 128, 128), BF)
+    held = (shapes[0], genc_held, shapes[2], gdec_held, shapes[4])
     results = pl.pallas_call(
-        functools.partial(kernel, stop),
+        kernel,
         out_shape=held,
-        in_specs=[inside, inside, outside, inside, outside, inside, outside, outside, outside, inside],
-        out_specs=[inside] * 5,
+        in_specs=[outside] * 10,
+        out_specs=[inside, outside, inside, outside, inside],
         scratch_shapes=[
+            vm((W, 256), BF),
+            vm((64, 256), jnp.int32),
+            vm((1, 128), F32),
+            vm((1, W), F32),
+            vm((W, 256), BF),
+            vm(genc_held.shape, BF),
+            vm(gdec_held.shape, BF),
             vm((NT, 16, 128), BF),
             vm((NT, 16, 128), BF),
+            vm((NZ, 16, 128), BF),
+            vm((NZ, 16, 128), BF),
             vm((NZ, 16, 128), BF),
             vm((NZ, 16, 128), BF),
             vm((2, 8, 2, NZ, 16, 128), BF),
@@ -764,14 +783,15 @@
             vm((NP, 8, FF), F32),
             vm((128, 2 * NZ * W), BF),
             vm((128, FF), BF),
-            dma((9,)), dma((9,)),
+            dma((11,)), dma((11,)),
             dma((7, NZ)), dma((7, NZ)),
-            dma((9, NT)), dma((9, NT)),
+            dma((12, NT)), dma((12, NT)),
             dma((4, MEM, 2)), dma((4, MEM)),
             dma((4 + 2 * NZ,)),
+            dma((15,)),
         ],
         compiler_params=pltpu.CompilerParams(
-            collective_id=cid, has_side_effects=True, vmem_limit_bytes=56 * 2**20
+            collective_id=1, has_side_effects=True, vmem_limit_bytes=56 * 2**20
         ),
         cost_estimate=pl.CostEstimate(flops=2 * 10**9, bytes_accessed=6 * 10**6, transcendentals=10**5),
         name="sae_step",

time: 125 us -> 125 us (level)
  no operation moved by 1% of the time
where the time goes in v4:
time: 125 us; the launch traced here: 124 us
  Pallas kernels  124 us (99%)
    pallas_call x1, Pallas kernels, step(): pl.pallas_call(kernel, out_shape=held, in_specs=[outside] * 10, out_specs...  121 us
    pallas_call x1, Pallas kernels, step(): pl.pallas_call(hand_on, out_shape=shapes, in_specs=[inside] * 5, out_spec...  3.21 us

profile of v4, /device:TPU:1, one launch (start us, length us, event | category | flops | bytes accessed | tf_op | source)
XLA Modules:
  0.0 124.5 jit_solution(6751151945730637521)
XLA Ops:
  0.6 120.6 %sae_step.1 = (bf16[16,112]{1,0:T(8,128)(2,1)}, bf16[2,16,112,128]{3,2,1,0:T(8,128)(2,1)}, f32[128]{0:T(128)}, bf16[16,2,128,128]{3,2,1,0:T(8,128)(2,1)}, f32[112]{0:T(128)}) custom-call(bf16[112,256]{1,0:T(8,128)(2,1)} %bitcast.8, s32[64,256]{1,0:T(8,128)} %bitcast.7, bf16[3584,128]{1,0:T(8,128)(2,1)} %wenc_ref.1, f32[1,128]{1,0:T(1,128)} %bitcast.10, ...), custom_call_target="tpu_custom_call" | custom-call | flops 2000000000 | bytes 6000000 | tf_op jit(solution)/shard_map/sae_step/pallas_call | solution.py:727
  121.3 3.2 %results.1 = (bf16[16,112]{1,0:T(8,128)(2,1)}, bf16[3584,128]{1,0:T(8,128)(2,1)}, f32[128]{0:T(128)}, bf16[128,3584]{1,0:T(8,128)(2,1)}, f32[112]{0:T(128)}) custom-call(bf16[16,112]{1,0:T(8,128)(2,1)} %get-tuple-element.10.out_in, bf16[2,16,112,128]{3,2,1,0:T(8,128)(2,1)} %get-tuple-element.11.genc_in, f32[128]{0:T(128)} %get-tuple-element.12.gencb_in, ...), custom_call_target="tpu_custom_call" | custom-call | tf_op jit(solution)/shard_map/results/pallas_call | solution.py:802
